TPU v7x, 32 devices: a whole 2x2x4 slice. The times are simulated.
32 devices in a mesh: state: 4 (over y, core), domain: 8 (over z, x).
Axes of the slice: x: 2, y: 2, z: 4, core: 2. Of those that a mesh axis runs over, the one named last changes fastest.
Arguments:
- orbitals: float32 [2, 4, 56, 25600], P(None, 'state', 'domain'), may hold values from -6 to 6
- occupation: float32 [4], P('state'), may hold values from 8e-07 to 3.2e-06
- potential: float32 [56, 25600], P('domain'), may hold values from 0 to 2
- background: float32 [56, 25600], P('domain'), may hold values from 0.005 to 270, as said below
- layer_start: int32 [9], replicated, may hold values from 0 to 40, as said below
Outputs:
- orbitals_next: float32 [2, 4, 56, 25600], P(None, 'state', 'domain')
- potential_next: float32 [56, 25600], P('domain')
Inputs may be any that keep to these rules, and one draw needn't show every extreme that they name: layer_start[d] - 5 d lies in 0..2, is 0 for the first and the last entry and 2 for the last domain's start, so each domain owns 3 to 7 layers and some domain owns exactly 7. `background`: positive.
All inputs are finite; a program needn't handle non-finite values.
Results may differ from a plain program's by a relative error of at most 0.000071.
Values sent between devices are 32-bit elements; how exact they have to be, the bound alone decides.
No kernel may reach another device: no remote copies, remote signals or barrier semaphores. Data moves between devices by JAX's collectives and lax.ppermute only.
A program may use at most 128 MiB of HBM per device.

v0:
```python
import functools
import math

import jax
import jax.numpy as jnp
import ml_dtypes
import numpy as np
from jax import lax
from jax.experimental import pallas as pl
from jax.experimental.pallas import tpu as pltpu
from jax.sharding import Mesh, PartitionSpec as P

SIDE = 160
SLAB = 5
TERMS = 4

HALO = TERMS
LANES = 128
SLOTS = 8
RUN = SIDE // 8
FLAT = SIDE * SIDE // LANES
STRIDE = FLAT // 8
WIDTH = 2 * LANES
BLOCK = 32
TALL = SIDE + 16

time_step = 0.3
four_pi = 4.0 * math.pi
two_pi = 2.0 * math.pi
highest = lax.Precision.HIGHEST
MEBI = 1024 * 1024
SMEM_SPEC = pl.BlockSpec(memory_space=pltpu.SMEM)
VMEM_SPEC = pl.BlockSpec(memory_space=pltpu.VMEM)
HBM_SPEC = pl.BlockSpec(memory_space=pltpu.HBM)


def hartley_table(count_cells):
    index_run = np.arange(count_cells)
    angles = (index_run[:, None] * index_run[None, :] % count_cells) * (2.0 * np.pi / count_cells)
    return np.cos(angles) + np.sin(angles)


def plane_order():
    rows = np.arange(SIDE)
    return RUN * (rows % 8) + rows // 8


def two_parts(table):
    table = table.astype(np.float32)
    high = table.astype(ml_dtypes.bfloat16)
    low = (table - high.astype(np.float32)).astype(ml_dtypes.bfloat16)
    return high, low


def tables_of_side():
    table = hartley_table(SIDE)
    along_z = np.zeros((WIDTH, WIDTH))
    along_z[:SIDE, :SIDE] = table
    high, low = two_parts(along_z)
    along_z = np.concatenate([high, high, low], axis=0)
    high, low = two_parts(table[:, plane_order()])
    into_y = np.concatenate([high, high, low], axis=1)
    high, low = two_parts(table[plane_order(), :])
    half = SIDE // 2
    halves = [slice(0, half), slice(half, SIDE)]
    out_of_y = np.stack([np.concatenate([high[:, at], high[:, at], low[:, at]], axis=1) for at in halves])
    return along_z, into_y, out_of_y


def circle_table():
    across = 2 * np.arange(SIDE, dtype=np.int64) - (SIDE - 1)
    return (across[:, None] ** 2 + across[None, :] ** 2).astype(np.int32)


def circle_plane():
    table = np.full((SIDE, WIDTH), 4 * SIDE * SIDE, np.int32)
    table[:, :SIDE] = circle_table()[plane_order()]
    return table


def mesh_points(x_row, circle, length_cells):
    room = ((length_cells - 2) ** 2 - (2 * x_row - (length_cells - 1)) ** 2) * (SIDE - 2) ** 2
    return (circle * (length_cells - 2) ** 2 <= room) & (circle < 4 * SIDE * SIDE)


def column_pieces(first, count):
    pieces = []
    column = first
    while column < first + count:
        row = column // SIDE
        stop = min((row + 1) * SIDE, first + count)
        pieces.append((row, column - row * SIDE, stop - row * SIDE))
        column = stop
    return pieces


def tile_rows(first, count):
    return pl.ds(first if isinstance(first, int) else pl.multiple_of(first, 8), count)


def eight(values):
    missing = jnp.zeros((SLOTS - values.shape[0], values.shape[1]), values.dtype)
    return jnp.concatenate([values, missing], axis=0)


def in_turns(first, last, size, body):
    turns = (last - first) // size
    if turns > 1:

        @pl.loop(0, turns)
        def _(turn):
            for index in range(size):
                body(first + turn * size + index)

        first += turns * size
    for index in range(first, last):
        body(index)


def to_plane(load, store):
    lane = lax.broadcasted_iota(jnp.int32, (8, LANES), 1)
    for step in range(RUN // 4):
        rows = [load(5 * step + part) for part in range(5)]
        store(4 * step, rows[0], rows[1])
        for part in range(1, 4):
            left = pltpu.roll(rows[part], LANES - 32 * part, 1)
            right = pltpu.roll(rows[part + 1], LANES - 32 * part, 1)
            store(4 * step + part, jnp.where(lane < LANES - 32 * part, left, right), right)


def to_flat(load, store):
    lane = lax.broadcasted_iota(jnp.int32, (8, LANES), 1)
    for step in range(RUN // 4):
        turned = []
        for part in range(4):
            low, high = load(4 * step + part)
            if part:
                low = pltpu.roll(low, 32 * part, 1)
                high = pltpu.roll(high, 32 * part, 1)
            turned.append((low, high))
        store(5 * step, turned[0][0])
        for part in range(1, 4):
            ended = 32 * (part - 1)
            values = jnp.where(lane < ended + 32, turned[part - 1][1], turned[part][0])
            if ended:
                values = jnp.where(lane < ended, turned[part - 1][0], values)
            store(5 * step + part, values)
        store(5 * step + 4, jnp.where(lane < 96, turned[3][0], turned[3][1]))


def chords():
    across = 2 * np.arange(SIDE, dtype=np.int64) - (SIDE - 1)
    room = (SIDE - 2) ** 2 - across**2
    return [max([w for w in range(1, SIDE // 2 + 1) if (2 * w - 1) ** 2 <= left], default=0) for left in room]


def chord_moves():
    moves = []
    packed = 0
    for row, half in enumerate(chords()):
        if half:
            moves.append((row * SIDE + SIDE // 2 - half, packed, 2 * half))
            packed += 2 * half
    return moves


def packed_tiles():
    _, start, length = chord_moves()[-1]
    return -(-(start + length) // LANES)


def move_lanes(moves, load, store):
    lane = lax.broadcasted_iota(jnp.int32, (8, LANES), 1)
    pieces = {}
    for source, target, length in moves:
        while length:
            size = min(length, LANES - source % LANES, LANES - target % LANES)
            pieces.setdefault(target // LANES, []).append((target % LANES, source // LANES, (target - source) % LANES))
            source, target, length = source + size, target + size, length - size
    loaded = {}
    turned = {}
    for tile in sorted(pieces):
        values = None
        for first, origin, shift in sorted(pieces[tile]):
            if origin not in loaded:
                loaded[origin] = load(origin)
            if (origin, shift) not in turned:
                turned[origin, shift] = pltpu.roll(loaded[origin], shift, 1) if shift else loaded[origin]
            piece = turned[origin, shift]
            values = piece if values is None else jnp.where(lane >= first, piece, values)
        store(tile, values)


def pack_chords(rows_ref, store):
    move_lanes(chord_moves(), lambda tile: rows_ref[pl.ds(tile, 8, stride=FLAT), :], store)


def unpack_chords(load, rows_ref):
    def store(tile, values):
        rows_ref[pl.ds(tile, 8, stride=FLAT), :] = values

    move_lanes([(target, source, length) for source, target, length in chord_moves()], load, store)


def parts_of(values):
    high = values.astype(jnp.bfloat16)
    low = (values - high.astype(jnp.float32)).astype(jnp.bfloat16)
    return high, low


def turn_z(values, table):
    high, low = parts_of(values)
    return jnp.dot(
        jnp.concatenate([high, low, high], axis=1), table, preferred_element_type=jnp.float32
    )


def turn_y(table, values):
    high, low = parts_of(values)
    return jnp.dot(
        table, jnp.concatenate([high, low, high], axis=0), preferred_element_type=jnp.float32
    )


def send_columns(planes_ref, slots, table_y, table_z, low_ref, high_ref):
    along_z = turn_z(planes_ref[:slots * SIDE, :], table_z)
    for slot in range(slots):
        rows = slice(slot * SIDE, (slot + 1) * SIDE)
        waves = turn_y(table_y, along_z[rows])
        low_ref[rows, :] = waves[:, :LANES]
        high_ref[rows, :] = waves[:, LANES:]
    low_ref[slots * SIDE:, :] = jnp.zeros(((SLOTS - slots) * SIDE, LANES), jnp.float32)
    high_ref[slots * SIDE:, :] = jnp.zeros(((SLOTS - slots) * SIDE, LANES), jnp.float32)


def chunk_of(low_ref, high_ref, first_row, pieces, extra):
    parts = []
    for row, start, stop in pieces:
        at = pl.ds(first_row + row, SLOTS, stride=SIDE)
        values = jnp.concatenate([low_ref[at, :], high_ref[at, :]], axis=1)
        parts.append(values[:, start:stop])
    return jnp.concatenate(parts + [extra], axis=1)


def layers_of(stored_ref, flat_ref):
    @pl.loop(0, FLAT // 8)
    def _(step):
        for part in range(8):
            lanes = pl.ds(pl.multiple_of((step * 8 + part) * LANES, LANES), LANES)
            flat_ref[pl.ds(step * 8 + part, SLOTS, stride=FLAT), :] = eight(stored_ref[:, lanes])


def place_of(start_ref):
    position = lax.axis_index("domain")
    return position, start_ref[position], start_ref[position + 1] - start_ref[position]


def started(sems, pairs):
    copies = [pltpu.make_async_copy(*pair, sems.at[index]) for index, pair in enumerate(pairs)]
    for made in copies:
        made.start()
    return copies


def layers_at(orbitals_ref, part, start, count):
    return orbitals_ref.at[part, pl.ds(pl.multiple_of(start * FLAT, 8), count * FLAT)]


def rows_at(ref, part, count):
    return ref.at[pl.ds(part * count * FLAT, count * FLAT)]


def pack_kernel(start_ref, orbitals_ref, up_ref, down_ref, up_rows_ref, down_rows_ref, up_buffer_ref,
                down_buffer_ref, in_sems, out_sems):
    _, _, thickness = place_of(start_ref)
    first = jnp.maximum(thickness - HALO, 0)
    arrivals = started(
        in_sems,
        [
            (layers_at(orbitals_ref, part, start, HALO), rows_at(rows_ref, part, HALO))
            for start, rows_ref in ((first, up_rows_ref), (0, down_rows_ref))
            for part in range(2)
        ],
    )
    departures = []
    for index, (rows_ref, buffer_ref, out_ref) in enumerate(
        ((up_rows_ref, up_buffer_ref, up_ref), (down_rows_ref, down_buffer_ref, down_ref))
    ):
        arrivals[2 * index].wait()
        arrivals[2 * index + 1].wait()

        def store(tile, values, buffer_ref=buffer_ref):
            buffer_ref[:, tile * LANES:(tile + 1) * LANES] = values

        pack_chords(rows_ref, store)
        departures.append(pltpu.make_async_copy(buffer_ref, out_ref, out_sems.at[index]))
        departures[-1].start()
    for made in departures:
        made.wait()


def pack_rest_kernel(start_ref, potential_ref, orbitals_ref, v_ref, up_far_ref, down_far_ref, flat_ref,
                     v_rows_ref, stored_ref, in_sems):
    _, _, thickness = place_of(start_ref)
    v_first = jnp.where(lax.axis_index("core") == 0, thickness - (HALO - 1), 0)
    arrivals = started(
        in_sems,
        [(potential_ref, stored_ref)]
        + [
            (layers_at(orbitals_ref, part, start, 1), rows_at(far_ref, part, 1))
            for start, far_ref in ((thickness - 1, up_far_ref), (0, down_far_ref))
            for part in range(2)
        ],
    )
    arrivals[0].wait()
    layers_of(stored_ref, flat_ref)
    for layer in range(HALO - 1):
        v_rows_ref[layer * FLAT:(layer + 1) * FLAT, :] = flat_ref[
            pl.ds(pl.multiple_of((v_first + layer) * FLAT, 8), FLAT), :
        ]

    def store_v(tile, values):
        for layer in range(HALO - 1):
            v_ref[layer, tile:tile + 1, :] = values[layer:layer + 1]

    pack_chords(v_rows_ref, store_v)
    for made in arrivals[1:]:
        made.wait()


def ions_kernel(count, length_cells, start_ref, background_ref, circle_ref, table_y_ref, table_z_ref,
                out_ref, flat_ref, planes_ref, low_ref, high_ref):
    _, own_start, thickness = place_of(start_ref)
    slots = background_ref.shape[0]
    groups, _, width = out_ref.shape
    layers_of(background_ref, flat_ref)

    def body(slot, total):
        def store(tile, low, high):
            rows = pl.ds(pl.multiple_of(slot * SIDE + tile * 8, 8), 8)
            planes_ref[rows, :LANES] = low
            planes_ref[rows, LANES:] = high

        to_plane(lambda k: flat_ref[pl.ds(slot * FLAT + k, 8, stride=STRIDE), :], store)
        rows = pl.ds(pl.multiple_of(slot * SIDE, 8), SIDE)
        inside = mesh_points(own_start + slot, circle_ref[...], length_cells) & (slot < thickness)
        values = jnp.where(inside, planes_ref[rows, :], 0.0)
        planes_ref[rows, :] = values
        return total + jnp.sum(values.reshape(RUN, 8, WIDTH), axis=0)

    total = lax.fori_loop(0, slots, body, jnp.zeros((8, WIDTH), jnp.float32))
    whole = jnp.broadcast_to(jnp.sum(total, keepdims=True), (SLOTS, LANES))[:, :width - count]
    send_columns(planes_ref, slots, table_y_ref[...], table_z_ref[...], low_ref, high_ref)
    core_rows = SIDE // lax.axis_size("core")
    first_row = lax.axis_index("core") * core_rows + lax.axis_index("row") * (core_rows // lax.axis_size("row"))
    for group in range(groups):
        out_ref[group] = chunk_of(low_ref, high_ref, first_row, column_pieces(group * count, count), whole)


def propagate_kernel(count, length_cells, start_ref, weight_ref, orbitals_ref, potential_ref, below_hbm_ref,
                     above_hbm_ref, below_far_hbm_ref, above_far_hbm_ref, v_hbm_ref, v_other_hbm_ref,
                     circle_ref, table_y_ref, table_z_ref, psi_ref, kept_ref, sent_ref, first_ref, second_ref,
                     third_ref, fourth_ref, sum_ref, centre_ref, beside_ref, flat_ref, planes_ref, low_ref,
                     high_ref, below_rows_ref, above_rows_ref, v_rows_ref, v_ref, v_other_ref, below_ref,
                     above_ref, below_far_ref, above_far_ref, in_sems, out_sem):
    arrivals = started(
        in_sems,
        [
            (v_hbm_ref, v_ref),
            (v_other_hbm_ref, v_other_ref),
            (below_hbm_ref, below_ref),
            (above_hbm_ref, above_ref),
            (below_far_hbm_ref, below_far_ref),
            (above_far_hbm_ref, above_far_ref),
        ],
    )
    position, own_start, thickness = place_of(start_ref)
    domains = lax.axis_size("domain")
    before = start_ref[jnp.maximum(position - 1, 0)]
    after = start_ref[jnp.minimum(position + 2, domains)]
    short_below = ((position > 0) & (own_start - before < HALO)).astype(jnp.int32)
    short_above = (position < domains - 1) & (after - own_start - thickness < HALO)
    weight = weight_ref[0]
    core = lax.axis_index("core")
    slots = orbitals_ref.shape[1]
    layers = slots + 2 * HALO
    devices, _, width = kept_ref.shape
    field_refs = (first_ref, second_ref, third_ref, fourth_ref)

    def field_layer(part, x_row):
        def store(tile, low, high):
            first_ref[part, x_row, 8 + 8 * tile:16 + 8 * tile, :LANES] = low
            first_ref[part, x_row, 8 + 8 * tile:16 + 8 * tile, LANES:] = high

        return store

    def potential_layer(x_row):
        def store(tile, low, high):
            centre_ref[x_row, 8 * tile:8 * tile + 8, :LANES] = low
            centre_ref[x_row, 8 * tile:8 * tile + 8, LANES:] = high

        return store

    def rows_from(ref, *at):
        return lambda k: ref[(*at, pl.ds(k, 8, stride=STRIDE), slice(None))]

    def layer_of(rows_ref, layer):
        return lambda k: rows_ref[pl.ds(layer * FLAT + k, 8, stride=STRIDE), :]

    layers_of(potential_ref, flat_ref)

    for slot in range(slots):
        for part in range(2):
            to_plane(rows_from(orbitals_ref, part, slot), field_layer(part, HALO + slot))
        to_plane(layer_of(flat_ref, slot), potential_layer(HALO + slot))

    for made in arrivals:
        made.wait()
    for packed_ref, rows_ref in ((below_ref, below_rows_ref), (above_ref, above_rows_ref)):
        unpack_chords(
            lambda tile, packed_ref=packed_ref: packed_ref[:, tile * LANES:(tile + 1) * LANES], rows_ref
        )
    unpack_chords(
        lambda tile: eight(
            jnp.concatenate([ref[:, tile, :] for ref in (v_ref, v_other_ref)], axis=0)
        ),
        v_rows_ref,
    )

    for layer in range(HALO - 1):
        lower = 1 + layer
        upper = HALO + thickness + layer
        to_plane(layer_of(v_rows_ref, layer), potential_layer(jnp.where(core == 0, lower, upper)))
        to_plane(layer_of(v_rows_ref, HALO - 1 + layer), potential_layer(jnp.where(core == 0, upper, lower)))
        for part in range(2):
            to_plane(
                layer_of(below_rows_ref, part * HALO + 1 + layer - short_below), field_layer(part, 1 + layer)
            )
            to_plane(
                layer_of(above_rows_ref, part * HALO + layer), field_layer(part, HALO + thickness + layer)
            )

    @pl.loop(0, 2)
    def _(part):
        last = 2 * HALO - 1 + thickness

        @pl.when(short_below > 0)
        def _():
            to_plane(layer_of(below_far_ref, part), field_layer(part, 0))

        @pl.when(short_below == 0)
        def _():
            to_plane(layer_of(below_rows_ref, part * HALO), field_layer(part, 0))

        @pl.when(short_above)
        def _():
            to_plane(layer_of(above_far_ref, part), field_layer(part, last))

        @pl.when(jnp.logical_not(short_above))
        def _():
            to_plane(layer_of(above_rows_ref, part * HALO + HALO - 1), field_layer(part, last))

    def wrap(field_ref, part, x_row, first, final):
        field_ref[part, x_row, :8, :] = pltpu.roll(final, 1, 0)
        field_ref[part, x_row, SIDE + 8:, :] = pltpu.roll(first, 7, 0)

    blocks = SIDE // BLOCK

    def confine(x_row):
        known = x_row < thickness + 2 * HALO
        ends = {}
        for block in range(blocks):
            rows = slice(block * BLOCK, (block + 1) * BLOCK)
            inner = slice(8 + block * BLOCK, 8 + (block + 1) * BLOCK)
            inside = mesh_points(own_start - HALO + x_row, circle_ref[rows, :], length_cells) & known
            centre_ref[x_row, rows, :] = jnp.where(
                inside, (3.0 + centre_ref[x_row, rows, :]) * time_step, 0.0
            )
            beside_ref[x_row, rows, :] = jnp.where(inside, 0.5 * time_step, 0.0)
            for part in range(2):
                field = jnp.where(inside, first_ref[part, x_row, inner, :], 0.0)
                first_ref[part, x_row, inner, :] = field
                ends[part, block] = field
        for part in range(2):
            wrap(first_ref, part, x_row, ends[part, 0][:8], ends[part, blocks - 1][BLOCK - 8:])

    in_turns(0, layers, 5, confine)

    def hamilton(term, part, x_row, block, centre, beside):
        field_ref = field_refs[term]
        tall = field_ref[part, x_row, block * BLOCK:block * BLOCK + BLOCK + 16, :]
        inner = slice(8 + block * BLOCK, 8 + (block + 1) * BLOCK)
        field = tall[8:8 + BLOCK]
        around = field_ref[part, x_row - 1, inner, :] + field_ref[part, x_row + 1, inner, :]
        around = around + (tall[:BLOCK] + tall[16:])
        around = around + (pltpu.roll(field, 1, 1) + pltpu.roll(field, WIDTH - 1, 1))
        return centre * field - beside * around

    for term in range(1, TERMS):

        def step(x_row, term=term):
            ends = {}
            for block in range(blocks):
                rows = slice(block * BLOCK, (block + 1) * BLOCK)
                inner = slice(8 + block * BLOCK, 8 + (block + 1) * BLOCK)
                centre = centre_ref[x_row, rows, :]
                beside = beside_ref[x_row, rows, :]
                for part in range(2):
                    field = hamilton(term - 1, part, x_row, block, centre, beside)
                    field_refs[term][part, x_row, inner, :] = field
                    ends[part, block] = field
            for part in range(2):
                wrap(field_refs[term], part, x_row, ends[part, 0][:8], ends[part, blocks - 1][BLOCK - 8:])

        in_turns(term, layers - term, 4, step)

    def finish(slot, total):
        x_row = HALO + slot
        owned = slot < thickness
        for block in range(SIDE // BLOCK):
            rows = slice(block * BLOCK, (block + 1) * BLOCK)
            inner = slice(8 + block * BLOCK, 8 + (block + 1) * BLOCK)
            centre = centre_ref[x_row, rows, :]
            beside = beside_ref[x_row, rows, :]
            density = jnp.zeros((BLOCK, WIDTH), jnp.float32)
            for part, sign in ((0, 1.0), (1, -1.0)):
                summed = first_ref[part, x_row, inner, :]
                summed = summed + sign * second_ref[1 - part, x_row, inner, :]
                summed = summed - (1.0 / 2.0) * third_ref[part, x_row, inner, :]
                summed = summed - (sign / 6.0) * fourth_ref[1 - part, x_row, inner, :]
                summed = summed + (1.0 / 24.0) * hamilton(3, part, x_row, block, centre, beside)
                summed = jnp.where(owned, summed, 0.0)
                sum_ref[part, slot, rows, :] = summed
                density = density + summed * summed
            density = weight * density
            planes_ref[tile_rows(slot * SIDE + block * BLOCK, BLOCK), :] = density
            total = total + jnp.sum(density.reshape(BLOCK // 8, 8, WIDTH), axis=0)

        return total

    total = lax.fori_loop(
        0, slots // 2, lambda pair, total: finish(2 * pair + 1, finish(2 * pair, total)), jnp.zeros((8, WIDTH), jnp.float32)
    )
    for slot in range(slots // 2 * 2, slots):
        total = finish(slot, total)
    departure = pltpu.make_async_copy(sum_ref, psi_ref, out_sem)
    departure.start()
    whole = jnp.broadcast_to(jnp.sum(total, keepdims=True), (SLOTS, LANES))[:, :width - count]
    send_columns(planes_ref, slots, table_y_ref[...], table_z_ref[...], low_ref, high_ref)
    core_rows = SIDE // 2
    first_row = core * core_rows
    for device in range(devices):
        pieces = column_pieces(device * count, count)
        kept_ref[device] = chunk_of(low_ref, high_ref, first_row, pieces, whole)
        sent_ref[device] = chunk_of(low_ref, high_ref, core_rows - first_row, pieces, whole)
    departure.wait()


def unpack_kernel(weight_ref, psi_ref, next_ref, density_kept_ref, density_sent_ref, density_ref):
    core = lax.axis_index("core")
    weight = weight_ref[0]
    slots = psi_ref.shape[1]

    def unpack(slot):
        for part in range(2):

            def load(tile, part=part):
                tall = psi_ref[part, slot, 8 * tile:8 * tile + 8, :]
                return tall[:, :LANES], tall[:, LANES:]

            def store(k, values, part=part):
                next_ref[part, slot, pl.ds(k, 8, stride=STRIDE), :] = values

            to_flat(load, store)
        real = next_ref[0, slot]
        imag = next_ref[1, slot]
        density_ref[slot] = weight * (real * real + imag * imag)

    in_turns(0, slots, 2, unpack)
    for slot in range(slots, SLOTS):
        density_ref[slot] = jnp.zeros((FLAT, LANES), jnp.float32)

    @pl.loop(0, SLOTS // 2)
    def _(slot):
        density_kept_ref[slot] = density_ref[core * (SLOTS // 2) + slot]
        density_sent_ref[slot] = density_ref[(1 - core) * (SLOTS // 2) + slot]


def wave_squared(index, count_cells):
    folded = jnp.where(2 * index <= count_cells, index, index - count_cells)
    wave_number = folded.astype(jnp.float32) * (two_pi / count_cells)
    return wave_number * wave_number


def coulomb_kernel(count, length_cells, start_ref, charge_ref, ions_ref, table_ref, out_ref):
    domains, _, width = ions_ref.shape
    states = charge_ref.shape[0] // domains
    device = (lax.axis_index("core") * states + lax.axis_index("row")) * domains + lax.axis_index("domain")
    charge = charge_ref[:domains]
    for state in range(1, states):
        charge = charge + charge_ref[state * domains:(state + 1) * domains]
    charge = charge.reshape(domains * SLOTS, width)
    ions = ions_ref[...].reshape(domains * SLOTS, width)
    first = lax.broadcasted_iota(jnp.int32, (domains * SLOTS, width), 0) % SLOTS == 0
    lane = lax.broadcasted_iota(jnp.int32, (domains * SLOTS, width), 1)
    chosen = first & (lane == count)
    electrons = jnp.sum(jnp.where(chosen, charge, 0.0), keepdims=True)
    ionic = jnp.sum(jnp.where(chosen, ions, 0.0), keepdims=True)
    charge = charge - (electrons / ionic) * ions
    layer = lax.broadcasted_iota(jnp.int32, (length_cells, domains * SLOTS), 0)
    place = lax.broadcasted_iota(jnp.int32, (length_cells, domains * SLOTS), 1)
    chosen_layer = jnp.full(layer.shape, -1, jnp.int32)
    for domain in range(domains):
        slot = place - domain * SLOTS
        here = (slot >= 0) & (slot < start_ref[domain + 1] - start_ref[domain])
        chosen_layer = jnp.where(here, start_ref[domain] + slot, chosen_layer)
    pick = (layer == chosen_layer).astype(jnp.float32)
    table = jnp.dot(table_ref[...], pick, precision=highest, preferred_element_type=jnp.float32)
    waves = jnp.dot(table, charge, precision=highest, preferred_element_type=jnp.float32)
    wave_x = lax.broadcasted_iota(jnp.int32, waves.shape, 0)
    column = device * count + lax.broadcasted_iota(jnp.int32, waves.shape, 1)
    wave_y = ((column.astype(jnp.float32) + 0.5) * (1.0 / SIDE)).astype(jnp.int32)
    wave_z = column - wave_y * SIDE
    squared = (
        wave_squared(wave_x, length_cells) + wave_squared(wave_y, SIDE) + wave_squared(wave_z, SIDE)
    )
    gain = jnp.where(squared > 0, four_pi / jnp.where(squared > 0, squared, 1.0), 0.0)
    waves = waves * (gain * (1.0 / (length_cells * SIDE * SIDE)))
    back = lax.dot_general(
        table, waves, (((0,), (0,)), ((), ())), precision=highest, preferred_element_type=jnp.float32
    )
    back = back.reshape(domains, SLOTS, width)
    for state in range(states):
        out_ref[state * domains:(state + 1) * domains] = back


def half_planes(count, source_ref, table_y, table_z, low_ref, high_ref, slots):
    half = SIDE // 2
    pieces = []
    for device in range(source_ref.shape[0]):
        column = 0
        for row, start, stop in column_pieces(device * count, count):
            values = source_ref[device, :, column:column + stop - start]
            column += stop - start
            if start > 0:
                pieces.append(values)
                values = jnp.concatenate(pieces, axis=1)
            if stop < SIDE:
                pieces = [values]
                continue
            pieces = []
            at = pl.ds(row, SLOTS, stride=half)
            low_ref[at, :] = values[:, :LANES]
            high_ref[at, :] = jnp.concatenate(
                [values[:, LANES:], jnp.zeros((SLOTS, WIDTH - SIDE), jnp.float32)], axis=1
            )
    used = slice(0, slots * half)
    along_z = turn_z(jnp.concatenate([low_ref[used, :], high_ref[used, :]], axis=1), table_z)
    return [turn_y(table_y, along_z[slot * half:(slot + 1) * half]) for slot in range(slots)]


def half_kernel(count, waves_ref, table_y_ref, table_z_ref, out_ref, low_ref, high_ref):
    table_y = table_y_ref[lax.axis_index("core")]
    slots = out_ref.shape[0] // SIDE
    planes = half_planes(count, waves_ref, table_y, table_z_ref[...], low_ref, high_ref, slots)
    for slot, plane in enumerate(planes):
        out_ref[slot * SIDE:(slot + 1) * SIDE, :] = plane


def field_kernel(count, length_cells, start_ref, others_ref, half_ref, density_ref, other_ref, circle_ref,
                 table_y_ref, table_z_ref, out_ref, low_ref, high_ref, planes_ref, flat_ref):
    _, own_start, thickness = place_of(start_ref)
    slots = out_ref.shape[0]
    core = lax.axis_index("core")
    planes = half_planes(count, others_ref, table_y_ref[1 - core], table_z_ref[...], low_ref, high_ref, slots)
    for slot, plane in enumerate(planes):
        rows = slice(slot * SIDE, (slot + 1) * SIDE)
        planes_ref[rows, :] = half_ref[rows, :] + plane

    def field(slot):
        def load(tile):
            tall = planes_ref[tile_rows(slot * SIDE + tile * 8, 8), :]
            return tall[:, :LANES], tall[:, LANES:]

        def store(k, values):
            flat_ref[pl.ds(slot * FLAT + k, 8, stride=STRIDE), :] = values

        to_flat(load, store)
        rows = tile_rows(slot * FLAT, FLAT)
        here = slot // (SLOTS // 2) == core
        kept_slot = slot % (SLOTS // 2)
        content = jnp.where(here, density_ref[kept_slot], other_ref[kept_slot]) * (3.0 / math.pi)
        positive = jnp.where(content > 0, content, 1.0)
        root = jnp.exp(jnp.log(positive) * (1.0 / 3.0))
        root = root - (root - positive / (root * root)) * (1.0 / 3.0)
        root = jnp.where(content > 0, root, 0.0)
        inside = mesh_points(own_start + slot, circle_ref[...], length_cells) & (slot < thickness)
        flat_ref[rows, :] = jnp.where(inside, flat_ref[rows, :] - root, 0.0)

    in_turns(0, slots, 4, field)

    @pl.loop(0, FLAT // 8)
    def _(step):
        for part in range(8):
            lanes = pl.ds(pl.multiple_of((step * 8 + part) * LANES, LANES), LANES)
            out_ref[:, lanes] = flat_ref[pl.ds(step * 8 + part, SLOTS, stride=FLAT), :][:slots]


def from_behind(value, steps):
    count = lax.axis_size("domain")
    leading, last = (max(0, -steps), min(count, count - steps))
    return lax.ppermute(value, "domain", [(source, source + steps) for source in range(leading, last)])


def swapped(value, axis):
    return lax.ppermute(value, axis, [(0, 1), (1, 0)])


def shards(orbitals, occupation, potential, background, layer_start):
    domains = lax.axis_size("domain")
    rows = lax.axis_size("row")
    devices = domains * rows
    length_cells = SLAB * domains
    layer_cap, plane = potential.shape
    count = plane // (2 * devices)
    width = -(-(count + 1) // LANES) * LANES
    circle = jnp.asarray(circle_plane())
    flat_circle = jnp.asarray(circle_table().reshape(FLAT, LANES))
    table_z, into_y, out_of_y = (jnp.asarray(table) for table in tables_of_side())
    table_x = jnp.asarray(hartley_table(length_cells).astype(np.float32))
    params = pltpu.CompilerParams(vmem_limit_bytes=16 * MEBI)
    large = pltpu.CompilerParams(vmem_limit_bytes=44 * MEBI)
    whole = pltpu.CompilerParams(vmem_limit_bytes=56 * MEBI)

    def f32(*shape):
        return jax.ShapeDtypeStruct(shape, jnp.float32)

    def scratch(*shape):
        return pltpu.VMEM(shape, jnp.float32)

    layers = orbitals.reshape(2, layer_cap, FLAT, LANES)
    packed = packed_tiles()
    outer = orbitals.reshape(2, layer_cap * FLAT, LANES)
    up, down = pl.pallas_call(
        pack_kernel,
        out_shape=(f32(2 * HALO, packed * LANES), f32(2 * HALO, packed * LANES)),
        in_specs=[SMEM_SPEC, HBM_SPEC],
        out_specs=(HBM_SPEC, HBM_SPEC),
        scratch_shapes=[
            scratch(2 * HALO * FLAT, LANES),
            scratch(2 * HALO * FLAT, LANES),
            scratch(2 * HALO, packed * LANES),
            scratch(2 * HALO, packed * LANES),
            pltpu.SemaphoreType.DMA((4,)),
            pltpu.SemaphoreType.DMA((2,)),
        ],
        compiler_params=whole,
        name="pack_halo",
    )(layer_start, outer)
    up, down, potential_rest, outer = lax.optimization_barrier((up, down, potential, outer))
    v_rows, up_far, down_far = pl.pallas_call(
        pack_rest_kernel,
        out_shape=(f32(HALO - 1, packed, LANES), f32(2 * FLAT, LANES), f32(2 * FLAT, LANES)),
        in_specs=[SMEM_SPEC, HBM_SPEC, HBM_SPEC],
        out_specs=(VMEM_SPEC,) * 3,
        scratch_shapes=[
            scratch(SLOTS * FLAT, LANES),
            scratch(SLOTS * FLAT, LANES),
            scratch(layer_cap, plane),
            pltpu.SemaphoreType.DMA((5,)),
        ],
        compiler_params=whole,
        cost_estimate=pl.CostEstimate(flops=0, transcendentals=0, bytes_accessed=30_000_000),
        name="pack_rest",
    )(layer_start, potential_rest, outer)
    v_rows = lax.ppermute(
        v_rows,
        ("core", "domain"),
        [(source, source + 1) for source in range(domains - 1)]
        + [(domains + source + 1, domains + source) for source in range(domains - 1)],
    )
    below = from_behind(up, 1)
    above = from_behind(down, -1)
    below_far = from_behind(up_far, 2)
    above_far = from_behind(down_far, -2)
    v_rows, below_far, above_far = lax.optimization_barrier((v_rows, below_far, above_far))
    v_others = swapped(v_rows, "core")

    ions = pl.pallas_call(
        functools.partial(ions_kernel, count, length_cells),
        out_shape=f32(domains, SLOTS, width),
        in_specs=[SMEM_SPEC] + [VMEM_SPEC] * 4,
        out_specs=VMEM_SPEC,
        scratch_shapes=[
            scratch(SLOTS * FLAT, LANES),
            scratch(layer_cap * SIDE, WIDTH),
            scratch(SLOTS * SIDE, LANES),
            scratch(SLOTS * SIDE, LANES),
        ],
        compiler_params=params,
        name="ion_waves",
    )(layer_start, background, circle, into_y, table_z)
    ions = lax.all_to_all(ions, "domain", split_axis=0, concat_axis=0, tiled=True)
    ions, below = lax.optimization_barrier((ions, below))

    span = layer_cap + 2 * HALO
    fields = (2, span, TALL, WIDTH)
    psi, kept, sent = pl.pallas_call(
        functools.partial(propagate_kernel, count, length_cells),
        out_shape=(
            pltpu.HBM((2, layer_cap, SIDE, WIDTH), jnp.float32),
            f32(devices, SLOTS, width),
            f32(devices, SLOTS, width),
        ),
        in_specs=[SMEM_SPEC, SMEM_SPEC, VMEM_SPEC, VMEM_SPEC] + [HBM_SPEC] * 6 + [VMEM_SPEC] * 3,
        out_specs=(HBM_SPEC, VMEM_SPEC, VMEM_SPEC),
        scratch_shapes=[scratch(*fields)] * TERMS
        + [
            scratch(2, layer_cap, SIDE, WIDTH),
            scratch(span, SIDE, WIDTH),
            scratch(span, SIDE, WIDTH),
            scratch(SLOTS * FLAT, LANES),
            scratch(layer_cap * SIDE, WIDTH),
            scratch(SLOTS * SIDE, LANES),
            scratch(SLOTS * SIDE, LANES),
            scratch(SLOTS * FLAT, LANES),
            scratch(SLOTS * FLAT, LANES),
            scratch(SLOTS * FLAT, LANES),
            scratch(HALO - 1, packed, LANES),
            scratch(HALO - 1, packed, LANES),
            scratch(2 * HALO, packed * LANES),
            scratch(2 * HALO, packed * LANES),
            scratch(2 * FLAT, LANES),
            scratch(2 * FLAT, LANES),
            pltpu.SemaphoreType.DMA((6,)),
            pltpu.SemaphoreType.DMA,
        ],
        compiler_params=large,
        name="propagate",
    )(layer_start, occupation, layers, potential, below, above, below_far, above_far, v_rows, v_others,
      circle, into_y, table_z)
    waves = kept + swapped(sent, "core")
    waves, psi = lax.optimization_barrier((waves, psi))
    waves = lax.all_to_all(waves, ("row", "domain"), split_axis=0, concat_axis=0, tiled=True)
    orbitals_next, density_kept, density_sent = pl.pallas_call(
        unpack_kernel,
        out_shape=(
            f32(2, layer_cap, FLAT, LANES),
            f32(SLOTS // 2, FLAT, LANES),
            f32(SLOTS // 2, FLAT, LANES),
        ),
        in_specs=[SMEM_SPEC, VMEM_SPEC],
        out_specs=(VMEM_SPEC,) * 3,
        scratch_shapes=[scratch(SLOTS, FLAT, LANES)],
        compiler_params=params,
        name="unpack",
    )(occupation, psi)
    density = density_kept + swapped(density_sent, "core")
    waves, density = lax.optimization_barrier((waves, density))
    other_density = swapped(density, "row")
    waves = pl.pallas_call(
        functools.partial(coulomb_kernel, count, length_cells),
        out_shape=f32(devices, SLOTS, width),
        in_specs=[SMEM_SPEC] + [VMEM_SPEC] * 3,
        out_specs=VMEM_SPEC,
        compiler_params=params,
        name="coulomb",
    )(layer_start, waves, ions, table_x)
    waves = lax.all_to_all(waves, ("row", "domain"), split_axis=0, concat_axis=0, tiled=True)
    waves, other_density = lax.optimization_barrier((waves, other_density))
    density = density + other_density
    other_density = swapped(density, "core")
    other_waves = swapped(waves, "core")
    half = [scratch(SLOTS * SIDE // 2, LANES), scratch(SLOTS * SIDE // 2, LANES)]
    planes = pl.pallas_call(
        functools.partial(half_kernel, count),
        out_shape=f32(layer_cap * SIDE, WIDTH),
        in_specs=[VMEM_SPEC] * 3,
        out_specs=VMEM_SPEC,
        scratch_shapes=half,
        compiler_params=params,
        name="half_field",
    )(waves, out_of_y, table_z)
    potential_next = pl.pallas_call(
        functools.partial(field_kernel, count, length_cells),
        out_shape=f32(layer_cap, plane),
        in_specs=[SMEM_SPEC] + [VMEM_SPEC] * 7,
        out_specs=VMEM_SPEC,
        scratch_shapes=half + [scratch(layer_cap * SIDE, WIDTH), scratch(SLOTS * FLAT, LANES)],
        compiler_params=params,
        name="field",
    )(layer_start, other_waves, planes, density, other_density, flat_circle, out_of_y, table_z)
    return orbitals_next.reshape(orbitals.shape), potential_next


def solution(mesh):
    domains = mesh.shape["domain"]
    split = Mesh(mesh.devices.reshape(-1, 2, domains), ("row", "core", "domain"))
    states = ("row", "core")
    return jax.shard_map(
        shards,
        mesh=split,
        in_specs=(
            P(None, states, "domain", None),
            P(states),
            P("domain", None),
            P("domain", None),
            P(),
        ),
        out_specs=(P(None, states, "domain", None), P("domain", None)),
        check_vma=False,
    )
```

profile of v0, /device:TPU:0, one launch (start us, length us, event | category | flops | bytes accessed | tf_op | source)
XLA Modules:
  0.0 113.6 jit_solution(8951708019559697308)
XLA Ops:
  0.6 3.4 %pack_halo.1 = (f32[8,19712]{1,0:T(8,128)}, f32[8,19712]{1,0:T(8,128)}) custom-call(s32[9]{0:T(128)} %start_ref.11, f32[2,1400,128]{2,1,0:T(8,128)} %bitcast.3), custom_call_target="tpu_custom_call" | custom-call | tf_op jit(solution)/shard_map/pack_halo/pallas_call | solution.py:744
  4.1 0.0 copy-start.1
  4.1 0.0 copy-start.4
  4.1 0.0 copy-start.6
  4.1 0.0 copy-start.7
  4.1 0.0 copy-start.10
  4.1 5.8 %collective-permute-start = (f32[8,19712]{1,0:T(8,128)}, f32[8,19712]{1,0:T(8,128)}, u32[]{:S(2)}, u32[]{:S(2)}) collective-permute-start(f32[8,19712]{1,0:T(8,128)} %get-tuple-element.30), channel_id=1, source_target_pairs={{0,1},{1,2},{2,3},{3,4},{4,5},{5,6},{6,7},{8,9},{9,10},{10,11},{11... | collective-permute-start | bytes 1892360 | tf_op jit(solution)/shard_map/ppermute | solution.py:712
  10.0 1.3 %collective-permute-start.1 = (f32[8,19712]{1,0:T(8,128)}, f32[8,19712]{1,0:T(8,128)}, u32[]{:S(2)}, u32[]{:S(2)}) collective-permute-start(f32[8,19712]{1,0:T(8,128)} %get-tuple-element.32), channel_id=1, source_target_pairs={{1,0},{2,1},{3,2},{4,3},{5,4},{6,5},{7,6},{9,8},{10,9},{11,10},{12... | collective-permute-start | bytes 1892360 | tf_op jit(solution)/shard_map/ppermute | solution.py:712
  11.2 0.0 copy-start.2
  11.3 3.7 %pack_rest.1 = (f32[3,154,128]{2,1,0:T(8,128)}, f32[400,128]{1,0:T(8,128)}, f32[400,128]{1,0:T(8,128)}) custom-call(s32[9]{0:T(128)} %start_ref.11, f32[7,25600]{1,0:T(8,128)} %potential_ref.2, f32[2,1400,128]{2,1,0:T(8,128)} %bitcast.4), custom_call_target="tpu_custom_call" | custom-call | bytes 30000000 | tf_op jit(solution)/shard_map/pack_rest/pallas_call | solution.py:761
  14.9 0.0 copy-start
  14.9 4.7 %collective-permute-start.2 = (f32[3,154,128]{2,1,0:T(8,128)}, f32[3,154,128]{2,1,0:T(8,128)S(1)}, u32[]{:S(2)}, u32[]{:S(2)}) collective-permute-start(f32[3,154,128]{2,1,0:T(8,128)} %get-tuple-element.35), channel_id=1, source_target_pairs={{0,1},{1,2},{2,3},{3,4},{4,5},{5,6},{6,7},{9,8},{10,9},{11,10},{12... | collective-permute-start | bytes 709640 | tf_op jit(solution)/shard_map/ppermute | solution.py:776
  19.6 3.6 %collective-permute-start.3 = (f32[400,128]{1,0:T(8,128)}, f32[400,128]{1,0:T(8,128)}, u32[]{:S(2)}, u32[]{:S(2)}) collective-permute-start(f32[400,128]{1,0:T(8,128)} %get-tuple-element.36), channel_id=1, source_target_pairs={{0,2},{1,3},{2,4},{3,5},{4,6},{5,7},{8,10},{9,11},{10,12},{11,13},... | collective-permute-start | bytes 614408 | tf_op jit(solution)/shard_map/ppermute | solution.py:712
  23.2 1.3 %collective-permute-start.4 = (f32[400,128]{1,0:T(8,128)}, f32[400,128]{1,0:T(8,128)}, u32[]{:S(2)}, u32[]{:S(2)}) collective-permute-start(f32[400,128]{1,0:T(8,128)} %get-tuple-element.37), channel_id=1, source_target_pairs={{2,0},{3,1},{4,2},{5,3},{6,4},{7,5},{10,8},{11,9},{12,10},{13,11},... | collective-permute-start | bytes 614408 | tf_op jit(solution)/shard_map/ppermute | solution.py:712
  24.5 4.3 %ion_waves.1 = f32[8,8,896]{2,1,0:T(8,128)} custom-call(s32[9]{0:T(128)S(1)} %copy-done.10, f32[7,25600]{1,0:T(8,128)S(1)} %copy-done.4, s32[160,256]{1,0:T(8,128)S(1)} %copy-done.7, bf16[160,480]{1,0:T(8,128)(2,1)S(1)} %copy-done.6, bf16[768,256]{1,0:T(8,128)(2,1)S(1)} %copy-done.1), custom_call_target="tpu_custom_call" | custom-call | tf_op jit(solution)/shard_map/ion_waves/pallas_call | solution.py:789
  28.8 6.8 %all-to-all-start = ((f32[8,8,896]{2,1,0:T(8,128)}), f32[8,8,896]{2,1,0:T(8,128)S(1)}, u32[]{:S(2)}, u32[]{:S(2)}) async-start(f32[8,8,896]{2,1,0:T(8,128)} %ion_waves.1), calls=%async_computation | async-start | bytes 458752 | tf_op jit(solution)/shard_map/all_to_all | solution.py:803
  35.6 0.0 collective-permute-done.3.below_far_hbm_ref
  35.6 0.0 collective-permute-done.4.above_far_hbm_ref
  35.6 8.2 %collective-permute-done.2.v_hbm_ref = f32[3,154,128]{2,1,0:T(8,128)S(1)} collective-permute-done((f32[3,154,128]{2,1,0:T(8,128)}, f32[3,154,128]{2,1,0:T(8,128)S(1)}, u32[]{:S(2)}, u32[]{:S(2)}) %collective-permute-start.2) | collective-permute-done | bytes 236576 | tf_op jit(solution)/shard_map/ppermute | solution.py:776
  43.8 0.0 collective-permute-start.5
  44.5 0.0 all-to-all-done.ions_ref
  44.5 0.0 collective-permute-done.below_hbm_ref
  44.5 1.0 collective-permute-done.5.v_other_hbm_ref
  45.5 0.0 collective-permute-done.1.above_hbm_ref
  45.5 16.9 %propagate.1 = (f32[2,7,160,256]{3,2,1,0:T(8,128)}, f32[16,8,896]{2,1,0:T(8,128)S(1)}, f32[16,8,896]{2,1,0:T(8,128)S(1)}) custom-call(s32[9]{0:T(128)S(1)} %copy-done.10, f32[1]{0:T(128)S(6)} %copy.18.weight_ref, f32[2,7,200,128]{3,2,1,0:T(8,128)S(1)} %bitcast.5, f32[7,25600]{1,0:T(8,128)S(1)} %copy-done.2, f32[8,19712]{1,0:T(8,128)} %collective-permute-done.below_hbm_ref, ...), custom_call_target="tpu_custom_call" | custom-call | tf_op jit(solution)/shard_map/propagate/pallas_call | solution.py:808
  62.4 0.2 collective-permute-start.6
  62.6 1.7 %collective-permute-done.6 = f32[16,8,896]{2,1,0:T(8,128)S(1)} collective-permute-done((f32[16,8,896]{2,1,0:T(8,128)S(1)}, f32[16,8,896]{2,1,0:T(8,128)S(1)}, u32[]{:S(2)}, u32[]{:S(2)}) %collective-permute-start.6) | collective-permute-done | bytes 458784 | tf_op jit(solution)/shard_map/ppermute | solution.py:716
  64.2 0.8 add.9
  65.1 7.2 %all-to-all-start.1 = ((f32[16,8,896]{2,1,0:T(8,128)}), f32[16,8,896]{2,1,0:T(8,128)S(1)}, u32[]{:S(2)}, u32[]{:S(2)}) async-start(f32[16,8,896]{2,1,0:T(8,128)} %add.9), calls=%async_computation.1 | async-start | bytes 917504 | tf_op jit(solution)/shard_map/all_to_all | solution.py:844
  72.3 1.6 %copy-done.3 = f32[2,7,160,256]{3,2,1,0:T(8,128)S(1)} copy-done((f32[2,7,160,256]{3,2,1,0:T(8,128)S(1)}, f32[2,7,160,256]{3,2,1,0:T(8,128)}, u32[]{:S(2)}) %copy-start.3) | copy-done | bytes 2293784
  73.9 2.0 %unpack.1 = (f32[2,7,200,128]{3,2,1,0:T(8,128)}, f32[4,200,128]{2,1,0:T(8,128)S(1)}, f32[4,200,128]{2,1,0:T(8,128)S(1)}) custom-call(f32[1]{0:T(128)S(6)} %copy.18.weight_ref, f32[2,7,160,256]{3,2,1,0:T(8,128)S(1)} %copy-done.3), custom_call_target="tpu_custom_call" | custom-call | tf_op jit(solution)/shard_map/unpack/pallas_call | solution.py:845
  75.9 0.1 collective-permute-start.7
  76.0 1.7 %collective-permute-done.7 = f32[4,200,128]{2,1,0:T(8,128)S(1)} collective-permute-done((f32[4,200,128]{2,1,0:T(8,128)S(1)}, f32[4,200,128]{2,1,0:T(8,128)S(1)}, u32[]{:S(2)}, u32[]{:S(2)}) %collective-permute-start.7) | collective-permute-done | bytes 409632 | tf_op jit(solution)/shard_map/ppermute | solution.py:716
  77.7 0.0 copy-start.5
  77.7 8.9 %all-to-all-done.1.charge_ref = f32[16,8,896]{2,1,0:T(8,128)S(1)} async-done(((f32[16,8,896]{2,1,0:T(8,128)}), f32[16,8,896]{2,1,0:T(8,128)S(1)}, u32[]{:S(2)}, u32[]{:S(2)}) %all-to-all-start.1) | async-done | bytes 458784 | tf_op jit(solution)/shard_map/all_to_all | solution.py:844
  86.6 2.1 %coulomb.1 = f32[16,8,896]{2,1,0:T(8,128)} custom-call(s32[9]{0:T(128)S(1)} %copy-done.10, f32[16,8,896]{2,1,0:T(8,128)S(1)} %all-to-all-done.1.charge_ref, f32[8,8,896]{2,1,0:T(8,128)S(1)} %all-to-all-done.ions_ref, f32[40,40]{1,0:T(8,128)S(1)} %copy-done.9), custom_call_target="tpu_custom_call" | custom-call | tf_op jit(solution)/shard_map/coulomb/pallas_call | solution.py:861
  88.7 3.8 %all-to-all-start.2 = ((f32[16,8,896]{2,1,0:T(8,128)}), f32[16,8,896]{2,1,0:T(8,128)S(1)}, u32[]{:S(2)}, u32[]{:S(2)}) async-start(f32[16,8,896]{2,1,0:T(8,128)} %coulomb.1), calls=%async_computation.2 | async-start | bytes 917504 | tf_op jit(solution)/shard_map/all_to_all | solution.py:869
  92.5 0.0 copy-start.8
  92.5 1.7 %collective-permute-start.8 = (f32[4,200,128]{2,1,0:T(8,128)S(1)}, f32[4,200,128]{2,1,0:T(8,128)S(1)}, u32[]{:S(2)}, u32[]{:S(2)}) collective-permute-start(f32[4,200,128]{2,1,0:T(8,128)S(1)} %add.10), channel_id=1, source_target_pairs={{0,16},{16,0},{1,17},{17,1},{2,18},{18,2},{3,19},{19,3},{4,20},{20... | collective-permute-start | bytes 1228808 | tf_op jit(solution)/shard_map/ppermute | solution.py:716
  94.2 13.7 %collective-permute-done.8 = f32[4,200,128]{2,1,0:T(8,128)S(1)} collective-permute-done((f32[4,200,128]{2,1,0:T(8,128)S(1)}, f32[4,200,128]{2,1,0:T(8,128)S(1)}, u32[]{:S(2)}, u32[]{:S(2)}) %collective-permute-start.8) | collective-permute-done | bytes 409632 | tf_op jit(solution)/shard_map/ppermute | solution.py:716
  107.8 0.0 all-to-all-done.2.waves_ref
  107.8 0.0 collective-permute-start.9
  107.8 0.1 add.11.density_ref
  107.9 0.6 collective-permute-start.10
  108.5 1.1 half_field.1.half_ref
  109.5 0.7 collective-permute-done.10.other_ref
  110.2 0.0 collective-permute-done.9.others_ref
  110.3 3.3 %field.1 = f32[7,25600]{1,0:T(8,128)} custom-call(s32[9]{0:T(128)S(1)} %copy-done.10, f32[16,8,896]{2,1,0:T(8,128)S(1)} %collective-permute-done.9.others_ref, f32[1120,256]{1,0:T(8,128)S(1)} %half_field.1.half_ref, f32[4,200,128]{2,1,0:T(8,128)S(1)} %add.11.density_ref, f32[4,200,128]{2,1,0:T(8,128)S(1)} %collective-permute-done.10.other_ref, ...), custom_call_target="tpu_custom_call" | custom-call | tf_op jit(solution)/shard_map/field/pallas_call | solution.py:884
  (13 shorter events, 0.1 us)
Async XLA Ops:
  4.1 20.4 %copy-start.1 = (bf16[768,256]{1,0:T(8,128)(2,1)S(1)}, bf16[768,256]{1,0:T(8,128)(2,1)}, u32[]{:S(2)}) copy-start(bf16[768,256]{1,0:T(8,128)(2,1)} %constant.14.clone.table_z_ref) | copy-start | bytes 1179652
  4.1 20.4 %copy-start.4 = (f32[7,25600]{1,0:T(8,128)S(1)}, f32[7,25600]{1,0:T(8,128)}, u32[]{:S(2)}) copy-start(f32[7,25600]{1,0:T(8,128)} %background_ref.1) | copy-start | bytes 2150404
  4.1 20.4 %copy-start.6 = (bf16[160,480]{1,0:T(8,128)(2,1)S(1)}, bf16[160,480]{1,0:T(8,128)(2,1)}, u32[]{:S(2)}) copy-start(bf16[160,480]{1,0:T(8,128)(2,1)} %constant.15.clone.table_y_ref) | copy-start | bytes 460804
  4.1 20.4 %copy-start.7 = (s32[160,256]{1,0:T(8,128)S(1)}, s32[160,256]{1,0:T(8,128)}, u32[]{:S(2)}) copy-start(s32[160,256]{1,0:T(8,128)} %constant.12.clone.circle_ref) | copy-start | bytes 491524
  4.1 20.4 %copy-start.10 = (s32[9]{0:T(128)S(1)}, s32[9]{0:T(128)}, u32[]{:S(2)}) copy-start(s32[9]{0:T(128)} %start_ref.11) | copy-start | bytes 112
  4.1 40.3 %collective-permute-start = (f32[8,19712]{1,0:T(8,128)}, f32[8,19712]{1,0:T(8,128)}, u32[]{:S(2)}, u32[]{:S(2)}) collective-permute-start(f32[8,19712]{1,0:T(8,128)} %get-tuple-element.30), channel_id=1, source_target_pairs={{0,1},{1,2},{2,3},{3,4},{4,5},{5,6},{6,7},{8,9},{9,10},{10,11},{11... | collective-permute-start | bytes 1892360 | tf_op jit(solution)/shard_map/ppermute | solution.py:712
  10.0 35.5 %collective-permute-start.1 = (f32[8,19712]{1,0:T(8,128)}, f32[8,19712]{1,0:T(8,128)}, u32[]{:S(2)}, u32[]{:S(2)}) collective-permute-start(f32[8,19712]{1,0:T(8,128)} %get-tuple-element.32), channel_id=1, source_target_pairs={{1,0},{2,1},{3,2},{4,3},{5,4},{6,5},{7,6},{9,8},{10,9},{11,10},{12... | collective-permute-start | bytes 1892360 | tf_op jit(solution)/shard_map/ppermute | solution.py:712
  11.2 34.2 %copy-start.2 = (f32[7,25600]{1,0:T(8,128)S(1)}, f32[7,25600]{1,0:T(8,128)}, u32[]{:S(2)}) copy-start(f32[7,25600]{1,0:T(8,128)} %potential_ref.2) | copy-start | bytes 2150404
  14.9 30.6 %copy-start = (f32[2,1,7,25600]{3,1,2,0:T(1,128)S(1)}, f32[2,1,7,25600]{3,1,2,0:T(1,128)}, u32[]{:S(2)}) copy-start(f32[2,1,7,25600]{3,1,2,0:T(1,128)} %param.11) | copy-start | bytes 4300804
  14.9 28.9 %collective-permute-start.2 = (f32[3,154,128]{2,1,0:T(8,128)}, f32[3,154,128]{2,1,0:T(8,128)S(1)}, u32[]{:S(2)}, u32[]{:S(2)}) collective-permute-start(f32[3,154,128]{2,1,0:T(8,128)} %get-tuple-element.35), channel_id=1, source_target_pairs={{0,1},{1,2},{2,3},{3,4},{4,5},{5,6},{6,7},{9,8},{10,9},{11,10},{12... | collective-permute-start | bytes 709640 | tf_op jit(solution)/shard_map/ppermute | solution.py:776
  19.6 16.0 %collective-permute-start.3 = (f32[400,128]{1,0:T(8,128)}, f32[400,128]{1,0:T(8,128)}, u32[]{:S(2)}, u32[]{:S(2)}) collective-permute-start(f32[400,128]{1,0:T(8,128)} %get-tuple-element.36), channel_id=1, source_target_pairs={{0,2},{1,3},{2,4},{3,5},{4,6},{5,7},{8,10},{9,11},{10,12},{11,13},... | collective-permute-start | bytes 614408 | tf_op jit(solution)/shard_map/ppermute | solution.py:712
  23.2 12.4 %collective-permute-start.4 = (f32[400,128]{1,0:T(8,128)}, f32[400,128]{1,0:T(8,128)}, u32[]{:S(2)}, u32[]{:S(2)}) collective-permute-start(f32[400,128]{1,0:T(8,128)} %get-tuple-element.37), channel_id=1, source_target_pairs={{2,0},{3,1},{4,2},{5,3},{6,4},{7,5},{10,8},{11,9},{12,10},{13,11},... | collective-permute-start | bytes 614408 | tf_op jit(solution)/shard_map/ppermute | solution.py:712
  28.8 15.6 %all-to-all-start = ((f32[8,8,896]{2,1,0:T(8,128)}), f32[8,8,896]{2,1,0:T(8,128)S(1)}, u32[]{:S(2)}, u32[]{:S(2)}) async-start(f32[8,8,896]{2,1,0:T(8,128)} %ion_waves.1), calls=%async_computation | async-start | bytes 458752 | tf_op jit(solution)/shard_map/all_to_all | solution.py:803
  43.8 1.6 %collective-permute-start.5 = (f32[3,154,128]{2,1,0:T(8,128)S(1)}, f32[3,154,128]{2,1,0:T(8,128)}, u32[]{:S(2)}, u32[]{:S(2)}) collective-permute-start(f32[3,154,128]{2,1,0:T(8,128)S(1)} %collective-permute-done.2.v_hbm_ref), channel_id=1, source_target_pairs={{0,8},{8,0},{1,9},{9,1},{2,10},{10,2},{3,11},{11,3},{4,12},{12,4},... | collective-permute-start | bytes 709640 | tf_op jit(solution)/shard_map/ppermute | solution.py:716
  62.4 1.9 %collective-permute-start.6 = (f32[16,8,896]{2,1,0:T(8,128)S(1)}, f32[16,8,896]{2,1,0:T(8,128)S(1)}, u32[]{:S(2)}, u32[]{:S(2)}) collective-permute-start(f32[16,8,896]{2,1,0:T(8,128)S(1)} %get-tuple-element.42), channel_id=1, source_target_pairs={{0,8},{8,0},{1,9},{9,1},{2,10},{10,2},{3,11},{11,3},{4,12},{12,4},... | collective-permute-start | bytes 1376264 | tf_op jit(solution)/shard_map/ppermute | solution.py:716
  65.1 21.5 %all-to-all-start.1 = ((f32[16,8,896]{2,1,0:T(8,128)}), f32[16,8,896]{2,1,0:T(8,128)S(1)}, u32[]{:S(2)}, u32[]{:S(2)}) async-start(f32[16,8,896]{2,1,0:T(8,128)} %add.9), calls=%async_computation.1 | async-start | bytes 917504 | tf_op jit(solution)/shard_map/all_to_all | solution.py:844
  72.3 1.6 %copy-start.3 = (f32[2,7,160,256]{3,2,1,0:T(8,128)S(1)}, f32[2,7,160,256]{3,2,1,0:T(8,128)}, u32[]{:S(2)}) copy-start(f32[2,7,160,256]{3,2,1,0:T(8,128)} %get-tuple-element.44.psi_ref) | copy-start | bytes 6881284
  73.9 12.7 %copy-start.9 = (f32[40,40]{1,0:T(8,128)S(1)}, f32[40,40]{1,0:T(8,128)}, u32[]{:S(2)}) copy-start(f32[40,40]{1,0:T(8,128)} %constant.17.clone.table_ref) | copy-start | bytes 19204
  75.9 1.7 %collective-permute-start.7 = (f32[4,200,128]{2,1,0:T(8,128)S(1)}, f32[4,200,128]{2,1,0:T(8,128)S(1)}, u32[]{:S(2)}, u32[]{:S(2)}) collective-permute-start(f32[4,200,128]{2,1,0:T(8,128)S(1)} %get-tuple-element.48), channel_id=1, source_target_pairs={{0,8},{8,0},{1,9},{9,1},{2,10},{10,2},{3,11},{11,3},{4,12},{12,4},... | collective-permute-start | bytes 1228808 | tf_op jit(solution)/shard_map/ppermute | solution.py:716
  77.7 30.8 %copy-start.5 = (bf16[2,160,240]{2,1,0:T(8,128)(2,1)S(1)}, bf16[2,160,240]{2,1,0:T(8,128)(2,1)}, u32[]{:S(2)}) copy-start(bf16[2,160,240]{2,1,0:T(8,128)(2,1)} %constant.16.clone.table_y_ref) | copy-start | bytes 460804
  88.7 19.2 %all-to-all-start.2 = ((f32[16,8,896]{2,1,0:T(8,128)}), f32[16,8,896]{2,1,0:T(8,128)S(1)}, u32[]{:S(2)}, u32[]{:S(2)}) async-start(f32[16,8,896]{2,1,0:T(8,128)} %coulomb.1), calls=%async_computation.2 | async-start | bytes 917504 | tf_op jit(solution)/shard_map/all_to_all | solution.py:869
  92.5 17.8 %copy-start.8 = (s32[200,128]{1,0:T(8,128)S(1)}, s32[200,128]{1,0:T(8,128)}, u32[]{:S(2)}) copy-start(s32[200,128]{1,0:T(8,128)} %constant.13.clone.circle_ref) | copy-start | bytes 307204
  92.5 15.3 %collective-permute-start.8 = (f32[4,200,128]{2,1,0:T(8,128)S(1)}, f32[4,200,128]{2,1,0:T(8,128)S(1)}, u32[]{:S(2)}, u32[]{:S(2)}) collective-permute-start(f32[4,200,128]{2,1,0:T(8,128)S(1)} %add.10), channel_id=1, source_target_pairs={{0,16},{16,0},{1,17},{17,1},{2,18},{18,2},{3,19},{19,3},{4,20},{20... | collective-permute-start | bytes 1228808 | tf_op jit(solution)/shard_map/ppermute | solution.py:716
  107.8 2.4 %collective-permute-start.9 = (f32[16,8,896]{2,1,0:T(8,128)S(1)}, f32[16,8,896]{2,1,0:T(8,128)S(1)}, u32[]{:S(2)}, u32[]{:S(2)}) collective-permute-start(f32[16,8,896]{2,1,0:T(8,128)S(1)} %all-to-all-done.2.waves_ref), channel_id=1, source_target_pairs={{0,8},{8,0},{1,9},{9,1},{2,10},{10,2},{3,11},{11,3},{4,12},{12,4},... | collective-permute-start | bytes 1376264 | tf_op jit(solution)/shard_map/ppermute | solution.py:716
  107.9 2.3 %collective-permute-start.10 = (f32[4,200,128]{2,1,0:T(8,128)S(1)}, f32[4,200,128]{2,1,0:T(8,128)S(1)}, u32[]{:S(2)}, u32[]{:S(2)}) collective-permute-start(f32[4,200,128]{2,1,0:T(8,128)S(1)} %add.11.density_ref), channel_id=1, source_target_pairs={{0,8},{8,0},{1,9},{9,1},{2,10},{10,2},{3,11},{11,3},{4,12},{12,4},... | collective-permute-start | bytes 1228808 | tf_op jit(solution)/shard_map/ppermute | solution.py:716
where the time goes:
time: 114 us
  starting transfers between devices  36.9 us (32%)
  Pallas kernels  36.7 us (32%)
  waiting for transfers between devices  35.8 us (31%)
  local copies, waits for them, and re-layouts  1.7 us (1%)
  between operations  1.52 us (1%)
    ppermute x6, waiting for transfers between devices, swapped(): return lax.ppermute(value, axis, [(0, 1), (1, 0)])  18.7 us
    pallas_call x1, Pallas kernels, shards(): pl.pallas_call(functools.partial(propagate_kernel, count, length_cells),...  16.9 us
    ppermute x4, starting transfers between devices, from_behind(): lax.ppermute(value, 'domain', [(source, source + steps) for source in ran...  11.9 us
    all_to_all x2, starting transfers between devices, shards(): lax.all_to_all(waves, ('row', 'domain'), split_axis=0, concat_axis=0, til...  11 us
    all_to_all x2, waiting for transfers between devices, shards(): lax.all_to_all(waves, ('row', 'domain'), split_axis=0, concat_axis=0, til...  8.92 us
    ppermute x1, waiting for transfers between devices, shards(): lax.ppermute(v_rows, ('core', 'domain'), [(source, source + 1) for source...  8.2 us
    all_to_all x1, starting transfers between devices, shards(): lax.all_to_all(ions, 'domain', split_axis=0, concat_axis=0, tiled=True)  6.75 us
    ppermute x1, starting transfers between devices, shards(): lax.ppermute(v_rows, ('core', 'domain'), [(source, source + 1) for source...  4.69 us
  transfers between devices with their start and end apart: 14, of which 7 were waited for; matrix products, arithmetic and copies ran while one was open for 0% of the time, Pallas kernels for 10%

commit v1 on v0

--- a/solution.py
+++ b/solution.py
@@ -59,7 +59,7 @@
     high, low = two_parts(along_z)
     along_z = np.concatenate([high, high, low], axis=0)
     high, low = two_parts(table[:, plane_order()])
-    into_y = np.concatenate([high, high, low], axis=1)
+    into_y = np.concatenate([high, high, low], axis=1).reshape(2, SIDE // 2, 3 * SIDE)
     high, low = two_parts(table[plane_order(), :])
     half = SIDE // 2
     halves = [slice(0, half), slice(half, SIDE)]
@@ -222,21 +222,21 @@
     )
 
 
-def send_columns(planes_ref, slots, table_y, table_z, low_ref, high_ref):
-    along_z = turn_z(planes_ref[:slots * SIDE, :], table_z)
+def half_columns(along_z, slots, table_y, low_ref, high_ref):
+    half = SIDE // 2
     for slot in range(slots):
-        rows = slice(slot * SIDE, (slot + 1) * SIDE)
-        waves = turn_y(table_y, along_z[rows])
+        rows = slice(slot * half, (slot + 1) * half)
+        waves = turn_y(table_y, along_z[slot * SIDE:(slot + 1) * SIDE])
         low_ref[rows, :] = waves[:, :LANES]
         high_ref[rows, :] = waves[:, LANES:]
-    low_ref[slots * SIDE:, :] = jnp.zeros(((SLOTS - slots) * SIDE, LANES), jnp.float32)
-    high_ref[slots * SIDE:, :] = jnp.zeros(((SLOTS - slots) * SIDE, LANES), jnp.float32)
+    low_ref[slots * half:, :] = jnp.zeros(((SLOTS - slots) * half, LANES), jnp.float32)
+    high_ref[slots * half:, :] = jnp.zeros(((SLOTS - slots) * half, LANES), jnp.float32)
 
 
 def chunk_of(low_ref, high_ref, first_row, pieces, extra):
     parts = []
     for row, start, stop in pieces:
-        at = pl.ds(first_row + row, SLOTS, stride=SIDE)
+        at = pl.ds(first_row + row, SLOTS, stride=SIDE // 2)
         values = jnp.concatenate([low_ref[at, :], high_ref[at, :]], axis=1)
         parts.append(values[:, start:stop])
     return jnp.concatenate(parts + [extra], axis=1)
@@ -350,16 +350,16 @@
 
     total = lax.fori_loop(0, slots, body, jnp.zeros((8, WIDTH), jnp.float32))
     whole = jnp.broadcast_to(jnp.sum(total, keepdims=True), (SLOTS, LANES))[:, :width - count]
-    send_columns(planes_ref, slots, table_y_ref[...], table_z_ref[...], low_ref, high_ref)
-    core_rows = SIDE // lax.axis_size("core")
-    first_row = lax.axis_index("core") * core_rows + lax.axis_index("row") * (core_rows // lax.axis_size("row"))
+    along_z = turn_z(planes_ref[...], table_z_ref[...])
+    half_columns(along_z, slots, table_y_ref[lax.axis_index("core")], low_ref, high_ref)
+    first_row = lax.axis_index("row") * (SIDE // 2 // lax.axis_size("row"))
     for group in range(groups):
         out_ref[group] = chunk_of(low_ref, high_ref, first_row, column_pieces(group * count, count), whole)
 
 
 def propagate_kernel(count, length_cells, start_ref, weight_ref, orbitals_ref, potential_ref, below_hbm_ref,
                      above_hbm_ref, below_far_hbm_ref, above_far_hbm_ref, v_hbm_ref, v_other_hbm_ref,
-                     circle_ref, table_y_ref, table_z_ref, psi_ref, kept_ref, sent_ref, first_ref, second_ref,
+                     circle_ref, table_y_ref, table_z_ref, psi_ref, along_ref, whole_ref, sent_ref, first_ref, second_ref,
                      third_ref, fourth_ref, sum_ref, centre_ref, beside_ref, flat_ref, planes_ref, low_ref,
                      high_ref, below_rows_ref, above_rows_ref, v_rows_ref, v_ref, v_other_ref, below_ref,
                      above_ref, below_far_ref, above_far_ref, in_sems, out_sem):
@@ -384,7 +384,7 @@
     core = lax.axis_index("core")
     slots = orbitals_ref.shape[1]
     layers = slots + 2 * HALO
-    devices, _, width = kept_ref.shape
+    devices, _, width = sent_ref.shape
     field_refs = (first_ref, second_ref, third_ref, fourth_ref)
 
     def field_layer(part, x_row):
@@ -545,15 +545,25 @@
         total = finish(slot, total)
     departure = pltpu.make_async_copy(sum_ref, psi_ref, out_sem)
     departure.start()
-    whole = jnp.broadcast_to(jnp.sum(total, keepdims=True), (SLOTS, LANES))[:, :width - count]
-    send_columns(planes_ref, slots, table_y_ref[...], table_z_ref[...], low_ref, high_ref)
-    core_rows = SIDE // 2
-    first_row = core * core_rows
+    whole = jnp.broadcast_to(jnp.sum(total, keepdims=True), (SLOTS, LANES))
+    whole_ref[...] = whole
+    along_z = turn_z(planes_ref[...], table_z_ref[...])
+    along_ref[...] = along_z
+    half_columns(along_z, slots, table_y_ref[1 - core], low_ref, high_ref)
     for device in range(devices):
-        pieces = column_pieces(device * count, count)
-        kept_ref[device] = chunk_of(low_ref, high_ref, first_row, pieces, whole)
-        sent_ref[device] = chunk_of(low_ref, high_ref, core_rows - first_row, pieces, whole)
+        sent_ref[device] = chunk_of(
+            low_ref, high_ref, 0, column_pieces(device * count, count), whole[:, :width - count]
+        )
     departure.wait()
+
+
+def kept_kernel(count, along_ref, whole_ref, table_y_ref, kept_ref, low_ref, high_ref):
+    devices, _, width = kept_ref.shape
+    slots = along_ref.shape[0] // SIDE
+    half_columns(along_ref[...], slots, table_y_ref[lax.axis_index("core")], low_ref, high_ref)
+    whole = whole_ref[...][:, :width - count]
+    for device in range(devices):
+        kept_ref[device] = chunk_of(low_ref, high_ref, 0, column_pieces(device * count, count), whole)
 
 
 def unpack_kernel(weight_ref, psi_ref, next_ref, density_kept_ref, density_sent_ref, density_ref):
@@ -794,8 +804,8 @@
         scratch_shapes=[
             scratch(SLOTS * FLAT, LANES),
             scratch(layer_cap * SIDE, WIDTH),
-            scratch(SLOTS * SIDE, LANES),
-            scratch(SLOTS * SIDE, LANES),
+            scratch(SLOTS * SIDE // 2, LANES),
+            scratch(SLOTS * SIDE // 2, LANES),
         ],
         compiler_params=params,
         name="ion_waves",
@@ -805,15 +815,16 @@
 
     span = layer_cap + 2 * HALO
     fields = (2, span, TALL, WIDTH)
-    psi, kept, sent = pl.pallas_call(
+    psi, along_z, whole_sum, sent = pl.pallas_call(
         functools.partial(propagate_kernel, count, length_cells),
         out_shape=(
             pltpu.HBM((2, layer_cap, SIDE, WIDTH), jnp.float32),
-            f32(devices, SLOTS, width),
+            f32(layer_cap * SIDE, WIDTH),
+            f32(SLOTS, LANES),
             f32(devices, SLOTS, width),
         ),
         in_specs=[SMEM_SPEC, SMEM_SPEC, VMEM_SPEC, VMEM_SPEC] + [HBM_SPEC] * 6 + [VMEM_SPEC] * 3,
-        out_specs=(HBM_SPEC, VMEM_SPEC, VMEM_SPEC),
+        out_specs=(HBM_SPEC, VMEM_SPEC, VMEM_SPEC, VMEM_SPEC),
         scratch_shapes=[scratch(*fields)] * TERMS
         + [
             scratch(2, layer_cap, SIDE, WIDTH),
@@ -821,8 +832,8 @@
             scratch(span, SIDE, WIDTH),
             scratch(SLOTS * FLAT, LANES),
             scratch(layer_cap * SIDE, WIDTH),
-            scratch(SLOTS * SIDE, LANES),
-            scratch(SLOTS * SIDE, LANES),
+            scratch(SLOTS * SIDE // 2, LANES),
+            scratch(SLOTS * SIDE // 2, LANES),
             scratch(SLOTS * FLAT, LANES),
             scratch(SLOTS * FLAT, LANES),
             scratch(SLOTS * FLAT, LANES),
@@ -839,6 +850,16 @@
         name="propagate",
     )(layer_start, occupation, layers, potential, below, above, below_far, above_far, v_rows, v_others,
       circle, into_y, table_z)
+    half = [scratch(SLOTS * SIDE // 2, LANES), scratch(SLOTS * SIDE // 2, LANES)]
+    kept = pl.pallas_call(
+        functools.partial(kept_kernel, count),
+        out_shape=f32(devices, SLOTS, width),
+        in_specs=[VMEM_SPEC] * 3,
+        out_specs=VMEM_SPEC,
+        scratch_shapes=half,
+        compiler_params=params,
+        name="kept_waves",
+    )(along_z, whole_sum, into_y)
     waves = kept + swapped(sent, "core")
     waves, psi = lax.optimization_barrier((waves, psi))
     waves = lax.all_to_all(waves, ("row", "domain"), split_axis=0, concat_axis=0, tiled=True)
@@ -871,7 +892,6 @@
     density = density + other_density
     other_density = swapped(density, "core")
     other_waves = swapped(waves, "core")
-    half = [scratch(SLOTS * SIDE // 2, LANES), scratch(SLOTS * SIDE // 2, LANES)]
     planes = pl.pallas_call(
         functools.partial(half_kernel, count),
         out_shape=f32(layer_cap * SIDE, WIDTH),

time: 114 us -> 112 us (0.982)
  Pallas kernels: 36.7 us -> 35.2 us
    pallas_call x1, Pallas kernels: 16.9 us -> 15 us  [shards(): pl.pallas_call(functools.partial(propagate_kernel, count, length_cells),...]
where the time goes in v1:
time: 112 us
  starting transfers between devices  36.9 us (33%)
  waiting for transfers between devices  35.5 us (32%)
  Pallas kernels  35.2 us (31%)
  local copies, waits for them, and re-layouts  1.7 us (2%)
  between operations  1.52 us (1%)
    ppermute x6, waiting for transfers between devices, swapped(): return lax.ppermute(value, axis, [(0, 1), (1, 0)])  18 us
    pallas_call x1, Pallas kernels, shards(): pl.pallas_call(functools.partial(propagate_kernel, count, length_cells),...  15 us
    ppermute x4, starting transfers between devices, from_behind(): lax.ppermute(value, 'domain', [(source, source + steps) for source in ran...  11.9 us
    all_to_all x2, starting transfers between devices, shards(): lax.all_to_all(waves, ('row', 'domain'), split_axis=0, concat_axis=0, til...  10.8 us
    all_to_all x2, waiting for transfers between devices, shards(): lax.all_to_all(waves, ('row', 'domain'), split_axis=0, concat_axis=0, til...  8.9 us
    ppermute x1, waiting for transfers between devices, shards(): lax.ppermute(v_rows, ('core', 'domain'), [(source, source + 1) for source...  8.51 us
    all_to_all x1, starting transfers between devices, shards(): lax.all_to_all(ions, 'domain', split_axis=0, concat_axis=0, tiled=True)  6.76 us
    ppermute x1, starting transfers between devices, shards(): lax.ppermute(v_rows, ('core', 'domain'), [(source, source + 1) for source...  4.69 us
  transfers between devices with their start and end apart: 14, of which 7 were waited for; matrix products, arithmetic and copies ran while one was open for 0% of the time, Pallas kernels for 10%

profile of v1, /device:TPU:0, one launch (start us, length us, event | category | flops | bytes accessed | tf_op | source)
XLA Modules:
  0.0 111.7 jit_solution(1485161250395713821)
XLA Ops:
  0.6 3.4 %pack_halo.1 = (f32[8,19712]{1,0:T(8,128)}, f32[8,19712]{1,0:T(8,128)}) custom-call(s32[9]{0:T(128)} %start_ref.11, f32[2,1400,128]{2,1,0:T(8,128)} %bitcast.3), custom_call_target="tpu_custom_call" | custom-call | tf_op jit(solution)/shard_map/pack_halo/pallas_call | solution.py:754
  4.1 0.0 copy-start.1
  4.1 0.0 copy-start.4
  4.1 0.0 copy-start.5
  4.1 0.0 copy-start.7
  4.1 0.0 copy-start.10
  4.1 5.8 %collective-permute-start = (f32[8,19712]{1,0:T(8,128)}, f32[8,19712]{1,0:T(8,128)}, u32[]{:S(2)}, u32[]{:S(2)}) collective-permute-start(f32[8,19712]{1,0:T(8,128)} %get-tuple-element.31), channel_id=1, source_target_pairs={{0,1},{1,2},{2,3},{3,4},{4,5},{5,6},{6,7},{8,9},{9,10},{10,11},{11... | collective-permute-start | bytes 1892360 | tf_op jit(solution)/shard_map/ppermute | solution.py:722
  10.0 1.3 %collective-permute-start.1 = (f32[8,19712]{1,0:T(8,128)}, f32[8,19712]{1,0:T(8,128)}, u32[]{:S(2)}, u32[]{:S(2)}) collective-permute-start(f32[8,19712]{1,0:T(8,128)} %get-tuple-element.33), channel_id=1, source_target_pairs={{1,0},{2,1},{3,2},{4,3},{5,4},{6,5},{7,6},{9,8},{10,9},{11,10},{12... | collective-permute-start | bytes 1892360 | tf_op jit(solution)/shard_map/ppermute | solution.py:722
  11.2 0.0 copy-start.2
  11.3 3.7 %pack_rest.1 = (f32[3,154,128]{2,1,0:T(8,128)}, f32[400,128]{1,0:T(8,128)}, f32[400,128]{1,0:T(8,128)}) custom-call(s32[9]{0:T(128)} %start_ref.11, f32[7,25600]{1,0:T(8,128)} %potential_ref.2, f32[2,1400,128]{2,1,0:T(8,128)} %bitcast.4), custom_call_target="tpu_custom_call" | custom-call | bytes 30000000 | tf_op jit(solution)/shard_map/pack_rest/pallas_call | solution.py:771
  14.9 0.0 copy-start
  14.9 4.7 %collective-permute-start.2 = (f32[3,154,128]{2,1,0:T(8,128)}, f32[3,154,128]{2,1,0:T(8,128)S(1)}, u32[]{:S(2)}, u32[]{:S(2)}) collective-permute-start(f32[3,154,128]{2,1,0:T(8,128)} %get-tuple-element.36), channel_id=1, source_target_pairs={{0,1},{1,2},{2,3},{3,4},{4,5},{5,6},{6,7},{9,8},{10,9},{11,10},{12... | collective-permute-start | bytes 709640 | tf_op jit(solution)/shard_map/ppermute | solution.py:786
  19.6 3.6 %collective-permute-start.3 = (f32[400,128]{1,0:T(8,128)}, f32[400,128]{1,0:T(8,128)}, u32[]{:S(2)}, u32[]{:S(2)}) collective-permute-start(f32[400,128]{1,0:T(8,128)} %get-tuple-element.37), channel_id=1, source_target_pairs={{0,2},{1,3},{2,4},{3,5},{4,6},{5,7},{8,10},{9,11},{10,12},{11,13},... | collective-permute-start | bytes 614408 | tf_op jit(solution)/shard_map/ppermute | solution.py:722
  23.2 1.3 %collective-permute-start.4 = (f32[400,128]{1,0:T(8,128)}, f32[400,128]{1,0:T(8,128)}, u32[]{:S(2)}, u32[]{:S(2)}) collective-permute-start(f32[400,128]{1,0:T(8,128)} %get-tuple-element.38), channel_id=1, source_target_pairs={{2,0},{3,1},{4,2},{5,3},{6,4},{7,5},{10,8},{11,9},{12,10},{13,11},... | collective-permute-start | bytes 614408 | tf_op jit(solution)/shard_map/ppermute | solution.py:722
  24.5 4.0 %ion_waves.1 = f32[8,8,896]{2,1,0:T(8,128)} custom-call(s32[9]{0:T(128)S(1)} %copy-done.10, f32[7,25600]{1,0:T(8,128)S(1)} %copy-done.5, s32[160,256]{1,0:T(8,128)S(1)} %copy-done.7, bf16[2,80,480]{2,1,0:T(8,128)(2,1)S(1)} %copy-done.4, bf16[768,256]{1,0:T(8,128)(2,1)S(1)} %copy-done.1), custom_call_target="tpu_custom_call" | custom-call | tf_op jit(solution)/shard_map/ion_waves/pallas_call | solution.py:799
  28.5 6.8 %all-to-all-start = ((f32[8,8,896]{2,1,0:T(8,128)}), f32[8,8,896]{2,1,0:T(8,128)S(1)}, u32[]{:S(2)}, u32[]{:S(2)}) async-start(f32[8,8,896]{2,1,0:T(8,128)} %ion_waves.1), calls=%async_computation | async-start | bytes 458752 | tf_op jit(solution)/shard_map/all_to_all | solution.py:813
  35.3 0.0 collective-permute-done.3.below_far_hbm_ref
  35.3 0.0 collective-permute-done.4.above_far_hbm_ref
  35.3 8.5 %collective-permute-done.2.v_hbm_ref = f32[3,154,128]{2,1,0:T(8,128)S(1)} collective-permute-done((f32[3,154,128]{2,1,0:T(8,128)}, f32[3,154,128]{2,1,0:T(8,128)S(1)}, u32[]{:S(2)}, u32[]{:S(2)}) %collective-permute-start.2) | collective-permute-done | bytes 236576 | tf_op jit(solution)/shard_map/ppermute | solution.py:786
  43.8 0.0 collective-permute-start.5
  44.5 0.0 all-to-all-done.ions_ref
  44.5 0.0 collective-permute-done.below_hbm_ref
  44.5 1.0 collective-permute-done.5.v_other_hbm_ref
  45.5 0.0 collective-permute-done.1.above_hbm_ref
  45.5 15.0 %propagate.1 = (f32[2,7,160,256]{3,2,1,0:T(8,128)}, f32[1120,256]{1,0:T(8,128)S(1)}, f32[8,128]{1,0:T(8,128)S(1)}, f32[16,8,896]{2,1,0:T(8,128)S(1)}) custom-call(s32[9]{0:T(128)S(1)} %copy-done.10, f32[1]{0:T(128)S(6)} %copy.18.weight_ref, f32[2,7,200,128]{3,2,1,0:T(8,128)S(1)} %bitcast.5, f32[7,25600]{1,0:T(8,128)S(1)} %copy-done.2, ...), custom_call_target="tpu_custom_call" | custom-call | tf_op jit(solution)/shard_map/propagate/pallas_call | solution.py:818
  60.5 0.2 collective-permute-start.6
  60.7 0.6 kept_waves.1
  61.3 1.0 collective-permute-done.6
  62.4 0.8 add.9
  63.2 7.2 %all-to-all-start.1 = ((f32[16,8,896]{2,1,0:T(8,128)}), f32[16,8,896]{2,1,0:T(8,128)S(1)}, u32[]{:S(2)}, u32[]{:S(2)}) async-start(f32[16,8,896]{2,1,0:T(8,128)} %add.9), calls=%async_computation.1 | async-start | bytes 917504 | tf_op jit(solution)/shard_map/all_to_all | solution.py:865
  70.4 1.6 %copy-done.3 = f32[2,7,160,256]{3,2,1,0:T(8,128)S(1)} copy-done((f32[2,7,160,256]{3,2,1,0:T(8,128)S(1)}, f32[2,7,160,256]{3,2,1,0:T(8,128)}, u32[]{:S(2)}) %copy-start.3) | copy-done | bytes 2293784
  72.1 2.0 %unpack.1 = (f32[2,7,200,128]{3,2,1,0:T(8,128)}, f32[4,200,128]{2,1,0:T(8,128)S(1)}, f32[4,200,128]{2,1,0:T(8,128)S(1)}) custom-call(f32[1]{0:T(128)S(6)} %copy.18.weight_ref, f32[2,7,160,256]{3,2,1,0:T(8,128)S(1)} %copy-done.3), custom_call_target="tpu_custom_call" | custom-call | tf_op jit(solution)/shard_map/unpack/pallas_call | solution.py:866
  74.0 0.1 collective-permute-start.7
  74.1 1.7 %collective-permute-done.7 = f32[4,200,128]{2,1,0:T(8,128)S(1)} collective-permute-done((f32[4,200,128]{2,1,0:T(8,128)S(1)}, f32[4,200,128]{2,1,0:T(8,128)S(1)}, u32[]{:S(2)}, u32[]{:S(2)}) %collective-permute-start.7) | collective-permute-done | bytes 409632 | tf_op jit(solution)/shard_map/ppermute | solution.py:726
  75.8 0.1 add.10
  75.8 0.0 copy-start.6
  75.8 8.9 %all-to-all-done.1.charge_ref = f32[16,8,896]{2,1,0:T(8,128)S(1)} async-done(((f32[16,8,896]{2,1,0:T(8,128)}), f32[16,8,896]{2,1,0:T(8,128)S(1)}, u32[]{:S(2)}, u32[]{:S(2)}) %all-to-all-start.1) | async-done | bytes 458784 | tf_op jit(solution)/shard_map/all_to_all | solution.py:865
  84.7 2.1 %coulomb.1 = f32[16,8,896]{2,1,0:T(8,128)} custom-call(s32[9]{0:T(128)S(1)} %copy-done.10, f32[16,8,896]{2,1,0:T(8,128)S(1)} %all-to-all-done.1.charge_ref, f32[8,8,896]{2,1,0:T(8,128)S(1)} %all-to-all-done.ions_ref, f32[40,40]{1,0:T(8,128)S(1)} %copy-done.9), custom_call_target="tpu_custom_call" | custom-call | tf_op jit(solution)/shard_map/coulomb/pallas_call | solution.py:882
  86.8 3.6 %all-to-all-start.2 = ((f32[16,8,896]{2,1,0:T(8,128)}), f32[16,8,896]{2,1,0:T(8,128)S(1)}, u32[]{:S(2)}, u32[]{:S(2)}) async-start(f32[16,8,896]{2,1,0:T(8,128)} %coulomb.1), calls=%async_computation.2 | async-start | bytes 917504 | tf_op jit(solution)/shard_map/all_to_all | solution.py:890
  90.4 0.0 copy-start.8
  90.4 1.9 %collective-permute-start.8 = (f32[4,200,128]{2,1,0:T(8,128)S(1)}, f32[4,200,128]{2,1,0:T(8,128)S(1)}, u32[]{:S(2)}, u32[]{:S(2)}) collective-permute-start(f32[4,200,128]{2,1,0:T(8,128)S(1)} %add.10), channel_id=1, source_target_pairs={{0,16},{16,0},{1,17},{17,1},{2,18},{18,2},{3,19},{19,3},{4,20},{20... | collective-permute-start | bytes 1228808 | tf_op jit(solution)/shard_map/ppermute | solution.py:726
  92.3 13.7 %collective-permute-done.8 = f32[4,200,128]{2,1,0:T(8,128)S(1)} collective-permute-done((f32[4,200,128]{2,1,0:T(8,128)S(1)}, f32[4,200,128]{2,1,0:T(8,128)S(1)}, u32[]{:S(2)}, u32[]{:S(2)}) %collective-permute-start.8) | collective-permute-done | bytes 409632 | tf_op jit(solution)/shard_map/ppermute | solution.py:726
  105.9 0.0 all-to-all-done.2.waves_ref
  106.0 0.0 collective-permute-start.9
  106.0 0.6 collective-permute-start.10
  106.6 1.1 half_field.1.half_ref
  107.6 0.7 collective-permute-done.10.other_ref
  108.4 3.3 %field.1 = f32[7,25600]{1,0:T(8,128)} custom-call(s32[9]{0:T(128)S(1)} %copy-done.10, f32[16,8,896]{2,1,0:T(8,128)S(1)} %collective-permute-done.9.others_ref, f32[1120,256]{1,0:T(8,128)S(1)} %half_field.1.half_ref, f32[4,200,128]{2,1,0:T(8,128)S(1)} %add.11.density_ref, f32[4,200,128]{2,1,0:T(8,128)S(1)} %collective-permute-done.10.other_ref, ...), custom_call_target="tpu_custom_call" | custom-call | tf_op jit(solution)/shard_map/field/pallas_call | solution.py:904
  (14 shorter events, 0.1 us)
Async XLA Ops:
  4.1 20.4 %copy-start.1 = (bf16[768,256]{1,0:T(8,128)(2,1)S(1)}, bf16[768,256]{1,0:T(8,128)(2,1)}, u32[]{:S(2)}) copy-start(bf16[768,256]{1,0:T(8,128)(2,1)} %constant.14.clone.table_z_ref) | copy-start | bytes 1179652
  4.1 20.4 %copy-start.4 = (bf16[2,80,480]{2,1,0:T(8,128)(2,1)S(1)}, bf16[2,80,480]{2,1,0:T(8,128)(2,1)}, u32[]{:S(2)}) copy-start(bf16[2,80,480]{2,1,0:T(8,128)(2,1)} %constant.15.clone.table_y_ref) | copy-start | bytes 460804
  4.1 20.4 %copy-start.5 = (f32[7,25600]{1,0:T(8,128)S(1)}, f32[7,25600]{1,0:T(8,128)}, u32[]{:S(2)}) copy-start(f32[7,25600]{1,0:T(8,128)} %background_ref.1) | copy-start | bytes 2150404
  4.1 20.4 %copy-start.7 = (s32[160,256]{1,0:T(8,128)S(1)}, s32[160,256]{1,0:T(8,128)}, u32[]{:S(2)}) copy-start(s32[160,256]{1,0:T(8,128)} %constant.12.clone.circle_ref) | copy-start | bytes 491524
  4.1 20.4 %copy-start.10 = (s32[9]{0:T(128)S(1)}, s32[9]{0:T(128)}, u32[]{:S(2)}) copy-start(s32[9]{0:T(128)} %start_ref.11) | copy-start | bytes 112
  4.1 40.3 %collective-permute-start = (f32[8,19712]{1,0:T(8,128)}, f32[8,19712]{1,0:T(8,128)}, u32[]{:S(2)}, u32[]{:S(2)}) collective-permute-start(f32[8,19712]{1,0:T(8,128)} %get-tuple-element.31), channel_id=1, source_target_pairs={{0,1},{1,2},{2,3},{3,4},{4,5},{5,6},{6,7},{8,9},{9,10},{10,11},{11... | collective-permute-start | bytes 1892360 | tf_op jit(solution)/shard_map/ppermute | solution.py:722
  10.0 35.5 %collective-permute-start.1 = (f32[8,19712]{1,0:T(8,128)}, f32[8,19712]{1,0:T(8,128)}, u32[]{:S(2)}, u32[]{:S(2)}) collective-permute-start(f32[8,19712]{1,0:T(8,128)} %get-tuple-element.33), channel_id=1, source_target_pairs={{1,0},{2,1},{3,2},{4,3},{5,4},{6,5},{7,6},{9,8},{10,9},{11,10},{12... | collective-permute-start | bytes 1892360 | tf_op jit(solution)/shard_map/ppermute | solution.py:722
  11.2 34.2 %copy-start.2 = (f32[7,25600]{1,0:T(8,128)S(1)}, f32[7,25600]{1,0:T(8,128)}, u32[]{:S(2)}) copy-start(f32[7,25600]{1,0:T(8,128)} %potential_ref.2) | copy-start | bytes 2150404
  14.9 30.6 %copy-start = (f32[2,1,7,25600]{3,1,2,0:T(1,128)S(1)}, f32[2,1,7,25600]{3,1,2,0:T(1,128)}, u32[]{:S(2)}) copy-start(f32[2,1,7,25600]{3,1,2,0:T(1,128)} %param.11) | copy-start | bytes 4300804
  14.9 28.9 %collective-permute-start.2 = (f32[3,154,128]{2,1,0:T(8,128)}, f32[3,154,128]{2,1,0:T(8,128)S(1)}, u32[]{:S(2)}, u32[]{:S(2)}) collective-permute-start(f32[3,154,128]{2,1,0:T(8,128)} %get-tuple-element.36), channel_id=1, source_target_pairs={{0,1},{1,2},{2,3},{3,4},{4,5},{5,6},{6,7},{9,8},{10,9},{11,10},{12... | collective-permute-start | bytes 709640 | tf_op jit(solution)/shard_map/ppermute | solution.py:786
  19.6 15.7 %collective-permute-start.3 = (f32[400,128]{1,0:T(8,128)}, f32[400,128]{1,0:T(8,128)}, u32[]{:S(2)}, u32[]{:S(2)}) collective-permute-start(f32[400,128]{1,0:T(8,128)} %get-tuple-element.37), channel_id=1, source_target_pairs={{0,2},{1,3},{2,4},{3,5},{4,6},{5,7},{8,10},{9,11},{10,12},{11,13},... | collective-permute-start | bytes 614408 | tf_op jit(solution)/shard_map/ppermute | solution.py:722
  23.2 12.1 %collective-permute-start.4 = (f32[400,128]{1,0:T(8,128)}, f32[400,128]{1,0:T(8,128)}, u32[]{:S(2)}, u32[]{:S(2)}) collective-permute-start(f32[400,128]{1,0:T(8,128)} %get-tuple-element.38), channel_id=1, source_target_pairs={{2,0},{3,1},{4,2},{5,3},{6,4},{7,5},{10,8},{11,9},{12,10},{13,11},... | collective-permute-start | bytes 614408 | tf_op jit(solution)/shard_map/ppermute | solution.py:722
  28.5 15.9 %all-to-all-start = ((f32[8,8,896]{2,1,0:T(8,128)}), f32[8,8,896]{2,1,0:T(8,128)S(1)}, u32[]{:S(2)}, u32[]{:S(2)}) async-start(f32[8,8,896]{2,1,0:T(8,128)} %ion_waves.1), calls=%async_computation | async-start | bytes 458752 | tf_op jit(solution)/shard_map/all_to_all | solution.py:813
  43.8 1.6 %collective-permute-start.5 = (f32[3,154,128]{2,1,0:T(8,128)S(1)}, f32[3,154,128]{2,1,0:T(8,128)}, u32[]{:S(2)}, u32[]{:S(2)}) collective-permute-start(f32[3,154,128]{2,1,0:T(8,128)S(1)} %collective-permute-done.2.v_hbm_ref), channel_id=1, source_target_pairs={{0,8},{8,0},{1,9},{9,1},{2,10},{10,2},{3,11},{11,3},{4,12},{12,4},... | collective-permute-start | bytes 709640 | tf_op jit(solution)/shard_map/ppermute | solution.py:726
  60.5 1.9 %collective-permute-start.6 = (f32[16,8,896]{2,1,0:T(8,128)S(1)}, f32[16,8,896]{2,1,0:T(8,128)S(1)}, u32[]{:S(2)}, u32[]{:S(2)}) collective-permute-start(f32[16,8,896]{2,1,0:T(8,128)S(1)} %get-tuple-element.44), channel_id=1, source_target_pairs={{0,8},{8,0},{1,9},{9,1},{2,10},{10,2},{3,11},{11,3},{4,12},{12,4},... | collective-permute-start | bytes 1376264 | tf_op jit(solution)/shard_map/ppermute | solution.py:726
  63.2 21.5 %all-to-all-start.1 = ((f32[16,8,896]{2,1,0:T(8,128)}), f32[16,8,896]{2,1,0:T(8,128)S(1)}, u32[]{:S(2)}, u32[]{:S(2)}) async-start(f32[16,8,896]{2,1,0:T(8,128)} %add.9), calls=%async_computation.1 | async-start | bytes 917504 | tf_op jit(solution)/shard_map/all_to_all | solution.py:865
  70.4 1.6 %copy-start.3 = (f32[2,7,160,256]{3,2,1,0:T(8,128)S(1)}, f32[2,7,160,256]{3,2,1,0:T(8,128)}, u32[]{:S(2)}) copy-start(f32[2,7,160,256]{3,2,1,0:T(8,128)} %get-tuple-element.46.psi_ref) | copy-start | bytes 6881284
  72.1 12.7 %copy-start.9 = (f32[40,40]{1,0:T(8,128)S(1)}, f32[40,40]{1,0:T(8,128)}, u32[]{:S(2)}) copy-start(f32[40,40]{1,0:T(8,128)} %constant.17.clone.table_ref) | copy-start | bytes 19204
  74.0 1.7 %collective-permute-start.7 = (f32[4,200,128]{2,1,0:T(8,128)S(1)}, f32[4,200,128]{2,1,0:T(8,128)S(1)}, u32[]{:S(2)}, u32[]{:S(2)}) collective-permute-start(f32[4,200,128]{2,1,0:T(8,128)S(1)} %get-tuple-element.50), channel_id=1, source_target_pairs={{0,8},{8,0},{1,9},{9,1},{2,10},{10,2},{3,11},{11,3},{4,12},{12,4},... | collective-permute-start | bytes 1228808 | tf_op jit(solution)/shard_map/ppermute | solution.py:726
  75.8 30.8 %copy-start.6 = (bf16[2,160,240]{2,1,0:T(8,128)(2,1)S(1)}, bf16[2,160,240]{2,1,0:T(8,128)(2,1)}, u32[]{:S(2)}) copy-start(bf16[2,160,240]{2,1,0:T(8,128)(2,1)} %constant.16.clone.table_y_ref) | copy-start | bytes 460804
  86.8 19.2 %all-to-all-start.2 = ((f32[16,8,896]{2,1,0:T(8,128)}), f32[16,8,896]{2,1,0:T(8,128)S(1)}, u32[]{:S(2)}, u32[]{:S(2)}) async-start(f32[16,8,896]{2,1,0:T(8,128)} %coulomb.1), calls=%async_computation.2 | async-start | bytes 917504 | tf_op jit(solution)/shard_map/all_to_all | solution.py:890
  90.4 18.0 %copy-start.8 = (s32[200,128]{1,0:T(8,128)S(1)}, s32[200,128]{1,0:T(8,128)}, u32[]{:S(2)}) copy-start(s32[200,128]{1,0:T(8,128)} %constant.13.clone.circle_ref) | copy-start | bytes 307204
  90.4 15.6 %collective-permute-start.8 = (f32[4,200,128]{2,1,0:T(8,128)S(1)}, f32[4,200,128]{2,1,0:T(8,128)S(1)}, u32[]{:S(2)}, u32[]{:S(2)}) collective-permute-start(f32[4,200,128]{2,1,0:T(8,128)S(1)} %add.10), channel_id=1, source_target_pairs={{0,16},{16,0},{1,17},{17,1},{2,18},{18,2},{3,19},{19,3},{4,20},{20... | collective-permute-start | bytes 1228808 | tf_op jit(solution)/shard_map/ppermute | solution.py:726
  106.0 2.4 %collective-permute-start.9 = (f32[16,8,896]{2,1,0:T(8,128)S(1)}, f32[16,8,896]{2,1,0:T(8,128)S(1)}, u32[]{:S(2)}, u32[]{:S(2)}) collective-permute-start(f32[16,8,896]{2,1,0:T(8,128)S(1)} %all-to-all-done.2.waves_ref), channel_id=1, source_target_pairs={{0,8},{8,0},{1,9},{9,1},{2,10},{10,2},{3,11},{11,3},{4,12},{12,4},... | collective-permute-start | bytes 1376264 | tf_op jit(solution)/shard_map/ppermute | solution.py:726
  106.0 2.4 %collective-permute-start.10 = (f32[4,200,128]{2,1,0:T(8,128)S(1)}, f32[4,200,128]{2,1,0:T(8,128)S(1)}, u32[]{:S(2)}, u32[]{:S(2)}) collective-permute-start(f32[4,200,128]{2,1,0:T(8,128)S(1)} %add.11.density_ref), channel_id=1, source_target_pairs={{0,8},{8,0},{1,9},{9,1},{2,10},{10,2},{3,11},{11,3},{4,12},{12,4},... | collective-permute-start | bytes 1228808 | tf_op jit(solution)/shard_map/ppermute | solution.py:726

commit v2 on v1

--- a/solution.py
+++ b/solution.py
@@ -21,7 +21,7 @@
 FLAT = SIDE * SIDE // LANES
 STRIDE = FLAT // 8
 WIDTH = 2 * LANES
-BLOCK = 32
+BLOCK = 40
 TALL = SIDE + 16
 
 time_step = 0.3
@@ -512,7 +512,7 @@
             for part in range(2):
                 wrap(field_refs[term], part, x_row, ends[part, 0][:8], ends[part, blocks - 1][BLOCK - 8:])
 
-        in_turns(term, layers - term, 4, step)
+        in_turns(term, layers - term, 6, step)
 
     def finish(slot, total):
         x_row = HALO + slot
@@ -538,10 +538,8 @@
 
         return total
 
-    total = lax.fori_loop(
-        0, slots // 2, lambda pair, total: finish(2 * pair + 1, finish(2 * pair, total)), jnp.zeros((8, WIDTH), jnp.float32)
-    )
-    for slot in range(slots // 2 * 2, slots):
+    total = jnp.zeros((8, WIDTH), jnp.float32)
+    for slot in range(slots):
         total = finish(slot, total)
     departure = pltpu.make_async_copy(sum_ref, psi_ref, out_sem)
     departure.start()

time: 112 us -> 113 us (level)
  no operation moved by 1% of the time
where the time goes in v2:
time: 113 us; the launch traced here: 112 us
  starting transfers between devices  36.9 us (33%)
  Pallas kernels  35.7 us (32%)
  waiting for transfers between devices  35.5 us (31%)
  local copies, waits for them, and re-layouts  1.7 us (2%)
  between operations  1.52 us (1%)
    ppermute x6, waiting for transfers between devices, swapped(): return lax.ppermute(value, axis, [(0, 1), (1, 0)])  18 us
    pallas_call x1, Pallas kernels, shards(): pl.pallas_call(functools.partial(propagate_kernel, count, length_cells),...  15.6 us
    ppermute x4, starting transfers between devices, from_behind(): lax.ppermute(value, 'domain', [(source, source + steps) for source in ran...  11.7 us
    all_to_all x2, starting transfers between devices, shards(): lax.all_to_all(waves, ('row', 'domain'), split_axis=0, concat_axis=0, til...  10.8 us
    all_to_all x2, waiting for transfers between devices, shards(): lax.all_to_all(waves, ('row', 'domain'), split_axis=0, concat_axis=0, til...  8.91 us
    ppermute x1, waiting for transfers between devices, shards(): lax.ppermute(v_rows, ('core', 'domain'), [(source, source + 1) for source...  8.51 us
    all_to_all x1, starting transfers between devices, shards(): lax.all_to_all(ions, 'domain', split_axis=0, concat_axis=0, tiled=True)  6.97 us
    ppermute x1, starting transfers between devices, shards(): lax.ppermute(v_rows, ('core', 'domain'), [(source, source + 1) for source...  4.69 us
  transfers between devices with their start and end apart: 14, of which 7 were waited for; matrix products, arithmetic and copies ran while one was open for 0% of the time, Pallas kernels for 10%

profile of v2, /device:TPU:0, one launch (start us, length us, event | category | flops | bytes accessed | tf_op | source)
XLA Modules:
  0.0 112.3 jit_solution(5562721218579592091)
XLA Ops:
  0.6 3.4 %pack_halo.1 = (f32[8,19712]{1,0:T(8,128)}, f32[8,19712]{1,0:T(8,128)}) custom-call(s32[9]{0:T(128)} %start_ref.11, f32[2,1400,128]{2,1,0:T(8,128)} %bitcast.3), custom_call_target="tpu_custom_call" | custom-call | tf_op jit(solution)/shard_map/pack_halo/pallas_call | solution.py:752
  4.1 0.0 copy-start.1
  4.1 0.0 copy-start.4
  4.1 0.0 copy-start.5
  4.1 0.0 copy-start.7
  4.1 0.0 copy-start.10
  4.1 5.8 %collective-permute-start = (f32[8,19712]{1,0:T(8,128)}, f32[8,19712]{1,0:T(8,128)}, u32[]{:S(2)}, u32[]{:S(2)}) collective-permute-start(f32[8,19712]{1,0:T(8,128)} %get-tuple-element.31), channel_id=1, source_target_pairs={{0,1},{1,2},{2,3},{3,4},{4,5},{5,6},{6,7},{8,9},{9,10},{10,11},{11... | collective-permute-start | bytes 1892360 | tf_op jit(solution)/shard_map/ppermute | solution.py:720
  10.0 1.3 %collective-permute-start.1 = (f32[8,19712]{1,0:T(8,128)}, f32[8,19712]{1,0:T(8,128)}, u32[]{:S(2)}, u32[]{:S(2)}) collective-permute-start(f32[8,19712]{1,0:T(8,128)} %get-tuple-element.33), channel_id=1, source_target_pairs={{1,0},{2,1},{3,2},{4,3},{5,4},{6,5},{7,6},{9,8},{10,9},{11,10},{12... | collective-permute-start | bytes 1892360 | tf_op jit(solution)/shard_map/ppermute | solution.py:720
  11.2 0.0 copy-start.2
  11.3 3.7 %pack_rest.1 = (f32[3,154,128]{2,1,0:T(8,128)}, f32[400,128]{1,0:T(8,128)}, f32[400,128]{1,0:T(8,128)}) custom-call(s32[9]{0:T(128)} %start_ref.11, f32[7,25600]{1,0:T(8,128)} %potential_ref.2, f32[2,1400,128]{2,1,0:T(8,128)} %bitcast.4), custom_call_target="tpu_custom_call" | custom-call | bytes 30000000 | tf_op jit(solution)/shard_map/pack_rest/pallas_call | solution.py:769
  14.9 0.0 copy-start
  14.9 4.7 %collective-permute-start.2 = (f32[3,154,128]{2,1,0:T(8,128)}, f32[3,154,128]{2,1,0:T(8,128)S(1)}, u32[]{:S(2)}, u32[]{:S(2)}) collective-permute-start(f32[3,154,128]{2,1,0:T(8,128)} %get-tuple-element.36), channel_id=1, source_target_pairs={{0,1},{1,2},{2,3},{3,4},{4,5},{5,6},{6,7},{9,8},{10,9},{11,10},{12... | collective-permute-start | bytes 709640 | tf_op jit(solution)/shard_map/ppermute | solution.py:784
  19.6 3.3 %collective-permute-start.3 = (f32[400,128]{1,0:T(8,128)}, f32[400,128]{1,0:T(8,128)}, u32[]{:S(2)}, u32[]{:S(2)}) collective-permute-start(f32[400,128]{1,0:T(8,128)} %get-tuple-element.37), channel_id=1, source_target_pairs={{0,2},{1,3},{2,4},{3,5},{4,6},{5,7},{8,10},{9,11},{10,12},{11,13},... | collective-permute-start | bytes 614408 | tf_op jit(solution)/shard_map/ppermute | solution.py:720
  23.0 1.3 %collective-permute-start.4 = (f32[400,128]{1,0:T(8,128)}, f32[400,128]{1,0:T(8,128)}, u32[]{:S(2)}, u32[]{:S(2)}) collective-permute-start(f32[400,128]{1,0:T(8,128)} %get-tuple-element.38), channel_id=1, source_target_pairs={{2,0},{3,1},{4,2},{5,3},{6,4},{7,5},{10,8},{11,9},{12,10},{13,11},... | collective-permute-start | bytes 614408 | tf_op jit(solution)/shard_map/ppermute | solution.py:720
  24.3 4.0 %ion_waves.1 = f32[8,8,896]{2,1,0:T(8,128)} custom-call(s32[9]{0:T(128)S(1)} %copy-done.10, f32[7,25600]{1,0:T(8,128)S(1)} %copy-done.5, s32[160,256]{1,0:T(8,128)S(1)} %copy-done.7, bf16[2,80,480]{2,1,0:T(8,128)(2,1)S(1)} %copy-done.4, bf16[768,256]{1,0:T(8,128)(2,1)S(1)} %copy-done.1), custom_call_target="tpu_custom_call" | custom-call | tf_op jit(solution)/shard_map/ion_waves/pallas_call | solution.py:797
  28.3 7.0 %all-to-all-start = ((f32[8,8,896]{2,1,0:T(8,128)}), f32[8,8,896]{2,1,0:T(8,128)S(1)}, u32[]{:S(2)}, u32[]{:S(2)}) async-start(f32[8,8,896]{2,1,0:T(8,128)} %ion_waves.1), calls=%async_computation | async-start | bytes 458752 | tf_op jit(solution)/shard_map/all_to_all | solution.py:811
  35.3 0.0 collective-permute-done.3.below_far_hbm_ref
  35.3 0.0 collective-permute-done.4.above_far_hbm_ref
  35.3 8.5 %collective-permute-done.2.v_hbm_ref = f32[3,154,128]{2,1,0:T(8,128)S(1)} collective-permute-done((f32[3,154,128]{2,1,0:T(8,128)}, f32[3,154,128]{2,1,0:T(8,128)S(1)}, u32[]{:S(2)}, u32[]{:S(2)}) %collective-permute-start.2) | collective-permute-done | bytes 236576 | tf_op jit(solution)/shard_map/ppermute | solution.py:784
  43.8 0.0 collective-permute-start.5
  44.5 0.0 all-to-all-done.ions_ref
  44.5 0.0 collective-permute-done.below_hbm_ref
  44.5 1.0 collective-permute-done.5.v_other_hbm_ref
  45.5 0.0 collective-permute-done.1.above_hbm_ref
  45.5 15.6 %propagate.1 = (f32[2,7,160,256]{3,2,1,0:T(8,128)}, f32[1120,256]{1,0:T(8,128)S(1)}, f32[8,128]{1,0:T(8,128)S(1)}, f32[16,8,896]{2,1,0:T(8,128)S(1)}) custom-call(s32[9]{0:T(128)S(1)} %copy-done.10, f32[1]{0:T(128)S(6)} %copy.18.weight_ref, f32[2,7,200,128]{3,2,1,0:T(8,128)S(1)} %bitcast.5, f32[7,25600]{1,0:T(8,128)S(1)} %copy-done.2, ...), custom_call_target="tpu_custom_call" | custom-call | tf_op jit(solution)/shard_map/propagate/pallas_call | solution.py:816
  61.1 0.2 collective-permute-start.6
  61.2 0.6 kept_waves.1
  61.9 1.0 collective-permute-done.6
  62.9 0.8 add.9
  63.8 7.2 %all-to-all-start.1 = ((f32[16,8,896]{2,1,0:T(8,128)}), f32[16,8,896]{2,1,0:T(8,128)S(1)}, u32[]{:S(2)}, u32[]{:S(2)}) async-start(f32[16,8,896]{2,1,0:T(8,128)} %add.9), calls=%async_computation.1 | async-start | bytes 917504 | tf_op jit(solution)/shard_map/all_to_all | solution.py:863
  71.0 1.6 %copy-done.3 = f32[2,7,160,256]{3,2,1,0:T(8,128)S(1)} copy-done((f32[2,7,160,256]{3,2,1,0:T(8,128)S(1)}, f32[2,7,160,256]{3,2,1,0:T(8,128)}, u32[]{:S(2)}) %copy-start.3) | copy-done | bytes 2293784
  72.6 2.0 %unpack.1 = (f32[2,7,200,128]{3,2,1,0:T(8,128)}, f32[4,200,128]{2,1,0:T(8,128)S(1)}, f32[4,200,128]{2,1,0:T(8,128)S(1)}) custom-call(f32[1]{0:T(128)S(6)} %copy.18.weight_ref, f32[2,7,160,256]{3,2,1,0:T(8,128)S(1)} %copy-done.3), custom_call_target="tpu_custom_call" | custom-call | tf_op jit(solution)/shard_map/unpack/pallas_call | solution.py:864
  74.6 0.1 collective-permute-start.7
  74.7 1.7 %collective-permute-done.7 = f32[4,200,128]{2,1,0:T(8,128)S(1)} collective-permute-done((f32[4,200,128]{2,1,0:T(8,128)S(1)}, f32[4,200,128]{2,1,0:T(8,128)S(1)}, u32[]{:S(2)}, u32[]{:S(2)}) %collective-permute-start.7) | collective-permute-done | bytes 409632 | tf_op jit(solution)/shard_map/ppermute | solution.py:724
  76.3 0.1 add.10
  76.4 0.0 copy-start.6
  76.4 8.9 %all-to-all-done.1.charge_ref = f32[16,8,896]{2,1,0:T(8,128)S(1)} async-done(((f32[16,8,896]{2,1,0:T(8,128)}), f32[16,8,896]{2,1,0:T(8,128)S(1)}, u32[]{:S(2)}, u32[]{:S(2)}) %all-to-all-start.1) | async-done | bytes 458784 | tf_op jit(solution)/shard_map/all_to_all | solution.py:863
  85.3 2.1 %coulomb.1 = f32[16,8,896]{2,1,0:T(8,128)} custom-call(s32[9]{0:T(128)S(1)} %copy-done.10, f32[16,8,896]{2,1,0:T(8,128)S(1)} %all-to-all-done.1.charge_ref, f32[8,8,896]{2,1,0:T(8,128)S(1)} %all-to-all-done.ions_ref, f32[40,40]{1,0:T(8,128)S(1)} %copy-done.9), custom_call_target="tpu_custom_call" | custom-call | tf_op jit(solution)/shard_map/coulomb/pallas_call | solution.py:880
  87.3 3.6 %all-to-all-start.2 = ((f32[16,8,896]{2,1,0:T(8,128)}), f32[16,8,896]{2,1,0:T(8,128)S(1)}, u32[]{:S(2)}, u32[]{:S(2)}) async-start(f32[16,8,896]{2,1,0:T(8,128)} %coulomb.1), calls=%async_computation.2 | async-start | bytes 917504 | tf_op jit(solution)/shard_map/all_to_all | solution.py:888
  90.9 0.0 copy-start.8
  90.9 1.9 %collective-permute-start.8 = (f32[4,200,128]{2,1,0:T(8,128)S(1)}, f32[4,200,128]{2,1,0:T(8,128)S(1)}, u32[]{:S(2)}, u32[]{:S(2)}) collective-permute-start(f32[4,200,128]{2,1,0:T(8,128)S(1)} %add.10), channel_id=1, source_target_pairs={{0,16},{16,0},{1,17},{17,1},{2,18},{18,2},{3,19},{19,3},{4,20},{20... | collective-permute-start | bytes 1228808 | tf_op jit(solution)/shard_map/ppermute | solution.py:724
  92.8 13.7 %collective-permute-done.8 = f32[4,200,128]{2,1,0:T(8,128)S(1)} collective-permute-done((f32[4,200,128]{2,1,0:T(8,128)S(1)}, f32[4,200,128]{2,1,0:T(8,128)S(1)}, u32[]{:S(2)}, u32[]{:S(2)}) %collective-permute-start.8) | collective-permute-done | bytes 409632 | tf_op jit(solution)/shard_map/ppermute | solution.py:724
  106.5 0.0 all-to-all-done.2.waves_ref
  106.5 0.0 collective-permute-start.9
  106.6 0.6 collective-permute-start.10
  107.1 1.1 half_field.1.half_ref
  108.2 0.7 collective-permute-done.10.other_ref
  108.9 3.3 %field.1 = f32[7,25600]{1,0:T(8,128)} custom-call(s32[9]{0:T(128)S(1)} %copy-done.10, f32[16,8,896]{2,1,0:T(8,128)S(1)} %collective-permute-done.9.others_ref, f32[1120,256]{1,0:T(8,128)S(1)} %half_field.1.half_ref, f32[4,200,128]{2,1,0:T(8,128)S(1)} %add.11.density_ref, f32[4,200,128]{2,1,0:T(8,128)S(1)} %collective-permute-done.10.other_ref, ...), custom_call_target="tpu_custom_call" | custom-call | tf_op jit(solution)/shard_map/field/pallas_call | solution.py:902
  (14 shorter events, 0.1 us)
Async XLA Ops:
  4.1 20.2 %copy-start.1 = (bf16[768,256]{1,0:T(8,128)(2,1)S(1)}, bf16[768,256]{1,0:T(8,128)(2,1)}, u32[]{:S(2)}) copy-start(bf16[768,256]{1,0:T(8,128)(2,1)} %constant.14.clone.table_z_ref) | copy-start | bytes 1179652
  4.1 20.2 %copy-start.4 = (bf16[2,80,480]{2,1,0:T(8,128)(2,1)S(1)}, bf16[2,80,480]{2,1,0:T(8,128)(2,1)}, u32[]{:S(2)}) copy-start(bf16[2,80,480]{2,1,0:T(8,128)(2,1)} %constant.15.clone.table_y_ref) | copy-start | bytes 460804
  4.1 20.2 %copy-start.5 = (f32[7,25600]{1,0:T(8,128)S(1)}, f32[7,25600]{1,0:T(8,128)}, u32[]{:S(2)}) copy-start(f32[7,25600]{1,0:T(8,128)} %background_ref.1) | copy-start | bytes 2150404
  4.1 20.2 %copy-start.7 = (s32[160,256]{1,0:T(8,128)S(1)}, s32[160,256]{1,0:T(8,128)}, u32[]{:S(2)}) copy-start(s32[160,256]{1,0:T(8,128)} %constant.12.clone.circle_ref) | copy-start | bytes 491524
  4.1 20.2 %copy-start.10 = (s32[9]{0:T(128)S(1)}, s32[9]{0:T(128)}, u32[]{:S(2)}) copy-start(s32[9]{0:T(128)} %start_ref.11) | copy-start | bytes 112
  4.1 40.3 %collective-permute-start = (f32[8,19712]{1,0:T(8,128)}, f32[8,19712]{1,0:T(8,128)}, u32[]{:S(2)}, u32[]{:S(2)}) collective-permute-start(f32[8,19712]{1,0:T(8,128)} %get-tuple-element.31), channel_id=1, source_target_pairs={{0,1},{1,2},{2,3},{3,4},{4,5},{5,6},{6,7},{8,9},{9,10},{10,11},{11... | collective-permute-start | bytes 1892360 | tf_op jit(solution)/shard_map/ppermute | solution.py:720
  10.0 35.5 %collective-permute-start.1 = (f32[8,19712]{1,0:T(8,128)}, f32[8,19712]{1,0:T(8,128)}, u32[]{:S(2)}, u32[]{:S(2)}) collective-permute-start(f32[8,19712]{1,0:T(8,128)} %get-tuple-element.33), channel_id=1, source_target_pairs={{1,0},{2,1},{3,2},{4,3},{5,4},{6,5},{7,6},{9,8},{10,9},{11,10},{12... | collective-permute-start | bytes 1892360 | tf_op jit(solution)/shard_map/ppermute | solution.py:720
  11.2 34.2 %copy-start.2 = (f32[7,25600]{1,0:T(8,128)S(1)}, f32[7,25600]{1,0:T(8,128)}, u32[]{:S(2)}) copy-start(f32[7,25600]{1,0:T(8,128)} %potential_ref.2) | copy-start | bytes 2150404
  14.9 30.6 %copy-start = (f32[2,1,7,25600]{3,1,2,0:T(1,128)S(1)}, f32[2,1,7,25600]{3,1,2,0:T(1,128)}, u32[]{:S(2)}) copy-start(f32[2,1,7,25600]{3,1,2,0:T(1,128)} %param.11) | copy-start | bytes 4300804
  14.9 28.9 %collective-permute-start.2 = (f32[3,154,128]{2,1,0:T(8,128)}, f32[3,154,128]{2,1,0:T(8,128)S(1)}, u32[]{:S(2)}, u32[]{:S(2)}) collective-permute-start(f32[3,154,128]{2,1,0:T(8,128)} %get-tuple-element.36), channel_id=1, source_target_pairs={{0,1},{1,2},{2,3},{3,4},{4,5},{5,6},{6,7},{9,8},{10,9},{11,10},{12... | collective-permute-start | bytes 709640 | tf_op jit(solution)/shard_map/ppermute | solution.py:784
  19.6 15.7 %collective-permute-start.3 = (f32[400,128]{1,0:T(8,128)}, f32[400,128]{1,0:T(8,128)}, u32[]{:S(2)}, u32[]{:S(2)}) collective-permute-start(f32[400,128]{1,0:T(8,128)} %get-tuple-element.37), channel_id=1, source_target_pairs={{0,2},{1,3},{2,4},{3,5},{4,6},{5,7},{8,10},{9,11},{10,12},{11,13},... | collective-permute-start | bytes 614408 | tf_op jit(solution)/shard_map/ppermute | solution.py:720
  23.0 12.3 %collective-permute-start.4 = (f32[400,128]{1,0:T(8,128)}, f32[400,128]{1,0:T(8,128)}, u32[]{:S(2)}, u32[]{:S(2)}) collective-permute-start(f32[400,128]{1,0:T(8,128)} %get-tuple-element.38), channel_id=1, source_target_pairs={{2,0},{3,1},{4,2},{5,3},{6,4},{7,5},{10,8},{11,9},{12,10},{13,11},... | collective-permute-start | bytes 614408 | tf_op jit(solution)/shard_map/ppermute | solution.py:720
  28.3 16.2 %all-to-all-start = ((f32[8,8,896]{2,1,0:T(8,128)}), f32[8,8,896]{2,1,0:T(8,128)S(1)}, u32[]{:S(2)}, u32[]{:S(2)}) async-start(f32[8,8,896]{2,1,0:T(8,128)} %ion_waves.1), calls=%async_computation | async-start | bytes 458752 | tf_op jit(solution)/shard_map/all_to_all | solution.py:811
  43.8 1.6 %collective-permute-start.5 = (f32[3,154,128]{2,1,0:T(8,128)S(1)}, f32[3,154,128]{2,1,0:T(8,128)}, u32[]{:S(2)}, u32[]{:S(2)}) collective-permute-start(f32[3,154,128]{2,1,0:T(8,128)S(1)} %collective-permute-done.2.v_hbm_ref), channel_id=1, source_target_pairs={{0,8},{8,0},{1,9},{9,1},{2,10},{10,2},{3,11},{11,3},{4,12},{12,4},... | collective-permute-start | bytes 709640 | tf_op jit(solution)/shard_map/ppermute | solution.py:724
  61.1 1.9 %collective-permute-start.6 = (f32[16,8,896]{2,1,0:T(8,128)S(1)}, f32[16,8,896]{2,1,0:T(8,128)S(1)}, u32[]{:S(2)}, u32[]{:S(2)}) collective-permute-start(f32[16,8,896]{2,1,0:T(8,128)S(1)} %get-tuple-element.44), channel_id=1, source_target_pairs={{0,8},{8,0},{1,9},{9,1},{2,10},{10,2},{3,11},{11,3},{4,12},{12,4},... | collective-permute-start | bytes 1376264 | tf_op jit(solution)/shard_map/ppermute | solution.py:724
  63.8 21.5 %all-to-all-start.1 = ((f32[16,8,896]{2,1,0:T(8,128)}), f32[16,8,896]{2,1,0:T(8,128)S(1)}, u32[]{:S(2)}, u32[]{:S(2)}) async-start(f32[16,8,896]{2,1,0:T(8,128)} %add.9), calls=%async_computation.1 | async-start | bytes 917504 | tf_op jit(solution)/shard_map/all_to_all | solution.py:863
  71.0 1.6 %copy-start.3 = (f32[2,7,160,256]{3,2,1,0:T(8,128)S(1)}, f32[2,7,160,256]{3,2,1,0:T(8,128)}, u32[]{:S(2)}) copy-start(f32[2,7,160,256]{3,2,1,0:T(8,128)} %get-tuple-element.46.psi_ref) | copy-start | bytes 6881284
  72.6 12.7 %copy-start.9 = (f32[40,40]{1,0:T(8,128)S(1)}, f32[40,40]{1,0:T(8,128)}, u32[]{:S(2)}) copy-start(f32[40,40]{1,0:T(8,128)} %constant.17.clone.table_ref) | copy-start | bytes 19204
  74.6 1.7 %collective-permute-start.7 = (f32[4,200,128]{2,1,0:T(8,128)S(1)}, f32[4,200,128]{2,1,0:T(8,128)S(1)}, u32[]{:S(2)}, u32[]{:S(2)}) collective-permute-start(f32[4,200,128]{2,1,0:T(8,128)S(1)} %get-tuple-element.50), channel_id=1, source_target_pairs={{0,8},{8,0},{1,9},{9,1},{2,10},{10,2},{3,11},{11,3},{4,12},{12,4},... | collective-permute-start | bytes 1228808 | tf_op jit(solution)/shard_map/ppermute | solution.py:724
  76.4 30.8 %copy-start.6 = (bf16[2,160,240]{2,1,0:T(8,128)(2,1)S(1)}, bf16[2,160,240]{2,1,0:T(8,128)(2,1)}, u32[]{:S(2)}) copy-start(bf16[2,160,240]{2,1,0:T(8,128)(2,1)} %constant.16.clone.table_y_ref) | copy-start | bytes 460804
  87.3 19.2 %all-to-all-start.2 = ((f32[16,8,896]{2,1,0:T(8,128)}), f32[16,8,896]{2,1,0:T(8,128)S(1)}, u32[]{:S(2)}, u32[]{:S(2)}) async-start(f32[16,8,896]{2,1,0:T(8,128)} %coulomb.1), calls=%async_computation.2 | async-start | bytes 917504 | tf_op jit(solution)/shard_map/all_to_all | solution.py:888
  90.9 18.0 %copy-start.8 = (s32[200,128]{1,0:T(8,128)S(1)}, s32[200,128]{1,0:T(8,128)}, u32[]{:S(2)}) copy-start(s32[200,128]{1,0:T(8,128)} %constant.13.clone.circle_ref) | copy-start | bytes 307204
  90.9 15.6 %collective-permute-start.8 = (f32[4,200,128]{2,1,0:T(8,128)S(1)}, f32[4,200,128]{2,1,0:T(8,128)S(1)}, u32[]{:S(2)}, u32[]{:S(2)}) collective-permute-start(f32[4,200,128]{2,1,0:T(8,128)S(1)} %add.10), channel_id=1, source_target_pairs={{0,16},{16,0},{1,17},{17,1},{2,18},{18,2},{3,19},{19,3},{4,20},{20... | collective-permute-start | bytes 1228808 | tf_op jit(solution)/shard_map/ppermute | solution.py:724
  106.5 2.4 %collective-permute-start.9 = (f32[16,8,896]{2,1,0:T(8,128)S(1)}, f32[16,8,896]{2,1,0:T(8,128)S(1)}, u32[]{:S(2)}, u32[]{:S(2)}) collective-permute-start(f32[16,8,896]{2,1,0:T(8,128)S(1)} %all-to-all-done.2.waves_ref), channel_id=1, source_target_pairs={{0,8},{8,0},{1,9},{9,1},{2,10},{10,2},{3,11},{11,3},{4,12},{12,4},... | collective-permute-start | bytes 1376264 | tf_op jit(solution)/shard_map/ppermute | solution.py:724
  106.6 2.4 %collective-permute-start.10 = (f32[4,200,128]{2,1,0:T(8,128)S(1)}, f32[4,200,128]{2,1,0:T(8,128)S(1)}, u32[]{:S(2)}, u32[]{:S(2)}) collective-permute-start(f32[4,200,128]{2,1,0:T(8,128)S(1)} %add.11.density_ref), channel_id=1, source_target_pairs={{0,8},{8,0},{1,9},{9,1},{2,10},{10,2},{3,11},{11,3},{4,12},{12,4},... | collective-permute-start | bytes 1228808 | tf_op jit(solution)/shard_map/ppermute | solution.py:724
